TPU v7x, 512 devices: a whole 4x4x16 slice. The times are simulated.
512 devices in a mesh: tile: 64 (over x, z), hid: 8 (over y, core).
Axes of the slice: x: 4, y: 4, z: 16, core: 2. Of those that a mesh axis runs over, the one named last changes fastest.
Arguments:
- nodes: bfloat16 [16384, 512], P('tile'), may hold values from -6 to 6
- edges: bfloat16 [49152, 512], P('tile'), may hold values from -6 to 6
- node_cotangent: bfloat16 [16384, 512], P('tile'), may hold values from -6 to 6
- edge_first: bfloat16 [1536, 512], P(None, 'hid'), may hold values from -0.15625 to 0.15625
- edge_second: bfloat16 [512, 512], P('hid'), may hold values from -0.25 to 0.25
- node_first: bfloat16 [1024, 512], P(None, 'hid'), may hold values from -0.1875 to 0.1875
- node_second: bfloat16 [512, 512], P('hid'), may hold values from -0.25 to 0.25
- sender: int32 [49152], P('tile'), may hold values from 0 to 767
- receiver_pos: int32 [49152], P('tile'), may hold values from 0 to 127
- block_tile: int32 [384], P('tile'), may hold values from 0 to 1
- live_blocks: int32 [64], P('tile'), may hold values from 3 to 6, as said below
- send_rows: int32 [64, 64, 8], P('tile'), may hold values from 0 to 255
Outputs:
- node_out: bfloat16 [16384, 512], P('tile')
- node_grad: bfloat16 [16384, 512], P('tile')
- edge_first_grad: float32 [1536, 512], P('tile', 'hid')
Inputs may be any that keep to these rules, and one draw needn't show every extreme that they name: Blocks 0 to live_blocks[d] - 1 of device d carry its edges, the later blocks none; some device has all 6 blocks live.
All inputs are finite; a program needn't handle non-finite values.
Results may differ from a plain program's by a relative error of at most 0.013.
Values may be sent and summed in bfloat16 or wider, within the bound.
No kernel may reach another device: no remote copies, remote signals or barrier semaphores. Data moves between devices by JAX's collectives and lax.ppermute only.
A program may use at most 64 MiB of HBM per device.

v0:
```python
import jax
import jax.numpy as jnp
from jax import lax
from jax.sharding import PartitionSpec as P

TILE = 128


epsilon = 1e-05


def layer_norm(values):
    centre = jnp.mean(values, axis=-1, keepdims=True)
    shifted = values - centre
    variance = jnp.mean(shifted * shifted, axis=-1, keepdims=True)
    return shifted * lax.rsqrt(variance + epsilon)


def silu_slope(preact):
    sigmoid_value = jax.nn.sigmoid(preact)
    return sigmoid_value * (1.0 + preact * (1.0 - sigmoid_value))


def tile_sum(values, receiver_pos, block_tile, tile_count):
    blocks = block_tile.shape[0]
    features = values.shape[1]
    positions = receiver_pos.reshape(blocks, TILE)
    onehot = (positions[:, :, None] == jnp.arange(TILE, dtype=jnp.int32)[None, None, :]).astype(
        jnp.bfloat16
    )
    per_block = jnp.einsum(
        "bep,bed->bpd",
        onehot,
        values.reshape(blocks, TILE, features),
        preferred_element_type=jnp.float32,
    )
    tile_hot = (block_tile[:, None] == jnp.arange(tile_count, dtype=jnp.int32)[None, :]).astype(
        jnp.float32
    )
    summed = jnp.einsum("bt,bpd->tpd", tile_hot, per_block, precision=lax.Precision.HIGHEST)
    return summed.reshape(tile_count * TILE, features)


def per_device(
    nodes,
    edges,
    node_cotangent,
    edge_first,
    edge_second,
    node_first,
    node_second,
    sender,
    receiver_pos,
    block_tile,
    live_blocks,
    send_rows,
):
    node_rows, features = nodes.shape
    edge_rows = edges.shape[0]
    blocks = block_tile.shape[0]
    tile_count = node_rows // TILE
    peer_count = send_rows.shape[1]
    slot_count = send_rows.shape[2]
    share_rows = edge_rows // lax.axis_size("hid")
    share_start = lax.axis_index("hid") * share_rows
    supply = jnp.take(nodes, send_rows[0].reshape(-1), axis=0).reshape(
        peer_count, slot_count, features
    )
    received = lax.all_to_all(supply, "tile", split_axis=0, concat_axis=0, tiled=True).reshape(
        peer_count * slot_count, features
    )
    node_table = jnp.concatenate([nodes, received], axis=0)
    receiver = jnp.repeat(block_tile, TILE) * TILE + receiver_pos
    live_rows = jnp.repeat(jnp.arange(blocks, dtype=jnp.int32) < live_blocks[0], TILE)
    stacked = jnp.concatenate(
        [edges, jnp.take(node_table, sender, axis=0), jnp.take(nodes, receiver, axis=0)], axis=1
    )
    preact = jnp.dot(stacked, edge_first, preferred_element_type=jnp.float32)
    hidden = jax.nn.silu(preact).astype(jnp.bfloat16)
    sum_share = lax.psum_scatter(
        jnp.dot(hidden, edge_second, preferred_element_type=jnp.float32),
        "hid",
        scatter_dimension=0,
        tiled=True,
    )
    norm_share, share_back = jax.vjp(layer_norm, sum_share)
    edge_share = lax.dynamic_slice_in_dim(edges, share_start, share_rows, 0)
    new_share = (edge_share.astype(jnp.float32) + norm_share).astype(jnp.bfloat16)
    edge_new = lax.all_gather(new_share, "hid", axis=0, tiled=True)
    masked_new = jnp.where(live_rows[:, None], edge_new, jnp.zeros_like(edge_new))
    aggregated = tile_sum(masked_new, receiver_pos, block_tile, tile_count)
    node_in = jnp.concatenate([nodes, aggregated.astype(jnp.bfloat16)], axis=1)
    preact_node = jnp.dot(node_in, node_first, preferred_element_type=jnp.float32)
    hidden_node = jax.nn.silu(preact_node).astype(jnp.bfloat16)
    node_sum = lax.psum(
        jnp.dot(hidden_node, node_second, preferred_element_type=jnp.float32), "hid"
    )
    node_norm, node_back = jax.vjp(layer_norm, node_sum)
    node_out = (nodes.astype(jnp.float32) + node_norm).astype(jnp.bfloat16)
    cotangent = node_cotangent.astype(jnp.float32)
    d_node_sum = node_back(cotangent)[0].astype(jnp.bfloat16)
    d_preact_node = (
        jnp.dot(d_node_sum, node_second.T, preferred_element_type=jnp.float32)
        * silu_slope(preact_node)
    ).astype(jnp.bfloat16)
    d_node_in = lax.psum(
        jnp.dot(d_preact_node, node_first.T, preferred_element_type=jnp.float32), "hid"
    )
    d_aggregated = d_node_in[:, features:].astype(jnp.bfloat16)
    live_share = lax.dynamic_slice_in_dim(live_rows, share_start, share_rows, 0)
    receiver_share = lax.dynamic_slice_in_dim(receiver, share_start, share_rows, 0)
    d_new_share = jnp.where(
        live_share[:, None],
        jnp.take(d_aggregated, receiver_share, axis=0).astype(jnp.float32),
        jnp.float32(0.0),
    )
    d_sum_share = share_back(d_new_share)[0].astype(jnp.bfloat16)
    d_edge_sum = lax.all_gather(d_sum_share, "hid", axis=0, tiled=True)
    d_preact = (
        jnp.dot(d_edge_sum, edge_second.T, preferred_element_type=jnp.float32) * silu_slope(preact)
    ).astype(jnp.bfloat16)
    edge_first_grad = lax.psum_scatter(
        lax.dot_general(
            stacked, d_preact, (((0,), (0,)), ((), ())), preferred_element_type=jnp.float32
        ),
        "tile",
        scatter_dimension=0,
        tiled=True,
    )
    tail_rows = edge_first[features:]
    d_stacked = lax.dot_general(
        d_preact, tail_rows, (((1,), (1,)), ((), ())), preferred_element_type=jnp.float32
    )
    table_grad = jax.ops.segment_sum(
        d_stacked[:, :features], sender, num_segments=node_rows + peer_count * slot_count
    )
    receiver_part = d_stacked[:, features:]
    upper_part = receiver_part.astype(jnp.bfloat16)
    lower_part = (receiver_part - upper_part.astype(jnp.float32)).astype(jnp.bfloat16)
    receiver_grad = tile_sum(upper_part, receiver_pos, block_tile, tile_count) + tile_sum(
        lower_part, receiver_pos, block_tile, tile_count
    )
    combined = jnp.concatenate(
        [table_grad[:node_rows] + receiver_grad, table_grad[node_rows:]], axis=0
    )
    combined = lax.psum(combined.astype(jnp.bfloat16), "hid").astype(jnp.float32)
    halo_part = combined[node_rows:].reshape(peer_count, slot_count, features)
    returned = lax.all_to_all(
        halo_part.astype(jnp.bfloat16), "tile", split_axis=0, concat_axis=0, tiled=True
    ).astype(halo_part.dtype)
    incoming = jax.ops.segment_sum(
        returned.reshape(peer_count * slot_count, features),
        send_rows[0].reshape(-1),
        num_segments=node_rows,
    )
    node_grad = (cotangent + d_node_in[:, :features] + combined[:node_rows] + incoming).astype(
        jnp.bfloat16
    )
    return (node_out, node_grad, edge_first_grad)


def solution(mesh):
    in_specs = (
        P("tile", None),
        P("tile", None),
        P("tile", None),
        P(None, "hid"),
        P("hid", None),
        P(None, "hid"),
        P("hid", None),
        P("tile"),
        P("tile"),
        P("tile"),
        P("tile"),
        P("tile", None, None),
    )
    out_specs = (P("tile", None), P("tile", None), P("tile", "hid"))
    return jax.shard_map(
        per_device, mesh=mesh, in_specs=in_specs, out_specs=out_specs, check_vma=False
    )
```

profile of v0, /device:TPU:1, one launch (start us, length us, event | category | flops | bytes accessed | tf_op | source)
XLA Modules:
  0.0 1011.8 jit_solution(9063805868112511684)
XLA Ops:
  7.2 0.7 compare_and_fusion.1
  7.9 0.8 copy.23
  8.9 3.0 gather_fusion
  11.9 0.9 bitcast_select_fusion
  12.9 19.1 %all-to-all-start = ((bf16[64,8,512]{2,1,0:T(8,128)(2,1)}), bf16[64,8,512]{2,1,0:T(8,128)(2,1)S(1)}, u32[]{:S(2)}, u32[]{:S(2)}) async-start(bf16[64,8,512]{2,1,0:T(8,128)(2,1)} %bitcast_select_fusion), calls=%async_computation | async-start | bytes 1048576 | tf_op jit(solution)/shard_map/all_to_all | solution.py:69
  32.2 2.7 gather_fusion.2
  35.1 26.3 %all-to-all-done = bf16[64,8,512]{2,1,0:T(8,128)(2,1)S(1)} async-done(((bf16[64,8,512]{2,1,0:T(8,128)(2,1)}), bf16[64,8,512]{2,1,0:T(8,128)(2,1)S(1)}, u32[]{:S(2)}, u32[]{:S(2)}) %all-to-all-start) | async-done | bytes 524320 | tf_op jit(solution)/shard_map/all_to_all | solution.py:69
  61.4 2.7 gather_fusion.1
  64.3 0.7 copy-done.14
  65.4 0.8 fusion.20
  66.3 1.6 fusion.40
  68.7 33.3 %reduce-scatter.5.cloned.1.call-done = f32[96,512]{1,0:T(8,128)} async-done(((f32[768,512]{1,0:T(8,128)}), f32[96,512]{1,0:T(8,128)}) %reduce-scatter.5.cloned.1.call-update) | async-done | bytes 196624 | tf_op jit(solution)/shard_map/reduce_scatter | solution.py:80
  102.0 1.0 reduce_sum.70
  103.1 1.1 multiply_reduce_fusion.2
  104.2 1.1 add_convert_fusion.5
  105.3 15.7 %all_gather.6 = bf16[768,512]{1,0:T(8,128)(2,1)S(1)} all-gather(bf16[96,512]{1,0:T(8,128)(2,1)S(1)} %add_convert_fusion.5), channel_id=1, replica_groups=mesh['tile'=64,'hid'=8] {'hid'}, dimensions={0}, use_global_device_ids=true | all-gather | bytes 884736 | tf_op jit(solution)/shard_map/all_gather | solution.py:89
  121.1 0.4 fusion.32
  121.5 1.9 fusion.11
  123.8 1.1 fusion.46
  124.9 74.1 %all-reduce.5.cloned.1.call-done = f32[256,512]{1,0:T(8,128)} async-done(((f32[256,512]{1,0:T(8,128)}), f32[256,512]{1,0:T(8,128)}) %all-reduce.5.cloned.1.call-update) | async-done | bytes 524304 | tf_op jit(solution)/shard_map/psum | solution.py:95
  199.0 1.2 reduce_sum.72
  200.3 1.3 fusion.22
  201.6 1.0 fusion.63
  202.6 1.8 fusion.16
  204.6 77.1 %all-reduce.7.cloned.1.call-done = f32[256,1024]{1,0:T(8,128)} async-done(((f32[256,1024]{1,0:T(8,128)}), f32[256,1024]{1,0:T(8,128)}) %all-reduce.7.cloned.1.call-update) | async-done | bytes 1048592 | tf_op jit(solution)/shard_map/psum | solution.py:106
  281.6 1.1 slice.76
  282.7 0.8 gather_fusion.3
  284.1 15.7 %all_gather.7 = bf16[768,512]{1,0:T(8,128)(2,1)S(1)} all-gather(bf16[96,512]{1,0:T(8,128)(2,1)S(1)} %add_convert_fusion.4), channel_id=1, replica_groups=mesh['tile'=64,'hid'=8] {'hid'}, dimensions={0}, use_global_device_ids=true | all-gather | bytes 884736 | tf_op jit(solution)/shard_map/all_gather | solution.py:118
  299.8 0.4 fusion.14
  300.1 0.6 copy-done.13
  300.8 0.6 fusion.38
  301.3 7.9 scatter_custom_fusion
  309.5 1.2 copy-done.4
  310.8 0.4 fusion.31
  311.1 0.4 fusion.30
  311.5 1.9 fusion
  313.4 2.0 fusion.8
  315.6 1.0 pad_maximum_fusion.4
  316.6 75.0 %all-reduce.9.cloned.1.call-done = bf16[768,512]{1,0:T(8,128)(2,1)} async-done(((bf16[768,512]{1,0:T(8,128)(2,1)}), bf16[768,512]{1,0:T(8,128)(2,1)}) %all-reduce.9.cloned.1.call-update) | async-done | bytes 786448 | tf_op jit(solution)/shard_map/psum | solution.py:146
  391.5 1.9 slice_bitcast_fusion
  393.4 14.9 %all-to-all-start.1 = ((bf16[64,8,512]{2,1,0:T(8,128)(2,1)}), bf16[64,8,512]{2,1,0:T(8,128)(2,1)S(1)}, u32[]{:S(2)}, u32[]{:S(2)}) async-start(bf16[64,8,512]{2,1,0:T(8,128)(2,1)} %slice_bitcast_fusion), calls=%async_computation.2 | async-start | bytes 1048576 | tf_op jit(solution)/shard_map/all_to_all | solution.py:148
  408.4 2.9 fusion.19
  411.3 0.8 reshape.193
  412.2 1.0 fusion.23
  413.2 22.7 %all-to-all-done.1 = bf16[64,8,512]{2,1,0:T(8,128)(2,1)S(1)} async-done(((bf16[64,8,512]{2,1,0:T(8,128)(2,1)}), bf16[64,8,512]{2,1,0:T(8,128)(2,1)S(1)}, u32[]{:S(2)}, u32[]{:S(2)}) %all-to-all-start.1) | async-done | bytes 524320 | tf_op jit(solution)/shard_map/all_to_all | solution.py:148
  435.9 4.1 scatter_custom_fusion.1
  440.0 0.7 convert_element_type.86
  440.8 564.5 %reduce-scatter.7.cloned.1.call-done = f32[24,64]{1,0:T(8,128)} async-done(((f32[1536,64]{1,0:T(8,128)}), f32[24,64]{1,0:T(8,128)}) %reduce-scatter.7.cloned.1.call-update) | async-done | bytes 6160
  (85 shorter events, 3.3 us)
Async XLA Ops:
  7.2 116.3 %copy-start = (bf16[1024,64]{0,1:T(8,128)(2,1)S(1)}, bf16[1024,64]{0,1:T(8,128)(2,1)}, u32[]{:S(2)}) copy-start(bf16[1024,64]{0,1:T(8,128)(2,1)} %param.17) | copy-start | bytes 393220
  8.7 3.2 copy-start.11
  11.9 20.1 %copy-start.20 = (s32[6]{0:T(128)S(1)}, s32[6]{0:T(128)}, u32[]{:S(2)}) copy-start(s32[6]{0:T(128)} %param.21) | copy-start | bytes 76
  11.9 20.2 %copy-start.16 = (s32[768]{0:T(1024)S(1)}, s32[768]{0:T(1024)}, u32[]{:S(2)}) copy-start(s32[768]{0:T(1024)} %param.20) | copy-start | bytes 9220
  11.9 20.2 %copy-start.1 = (bf16[256,512]{1,0:T(8,128)(2,1)S(1)}, bf16[256,512]{1,0:T(8,128)(2,1)}, u32[]{:S(2)}) copy-start(bf16[256,512]{1,0:T(8,128)(2,1)} %param.12) | copy-start | bytes 786436
  12.9 48.5 %all-to-all-start = ((bf16[64,8,512]{2,1,0:T(8,128)(2,1)}), bf16[64,8,512]{2,1,0:T(8,128)(2,1)S(1)}, u32[]{:S(2)}, u32[]{:S(2)}) async-start(bf16[64,8,512]{2,1,0:T(8,128)(2,1)} %bitcast_select_fusion), calls=%async_computation | async-start | bytes 1048576 | tf_op jit(solution)/shard_map/all_to_all | solution.py:69
  32.0 70.0 %reduce-scatter.5.cloned.1.call-start = ((), (), s32[]{:S(2)}) async-start(), calls=%async_computation.4 | async-start | bytes 1769472 | tf_op jit(solution)/shard_map/reduce_scatter | solution.py:80
  32.2 2.7 copy-start.18
  35.1 29.2 %copy-start.6 = (bf16[768,512]{1,0:T(8,128)(2,1)}, bf16[768,512]{1,0:T(8,128)(2,1)S(1)}, u32[]{:S(2)}) copy-start(bf16[768,512]{1,0:T(8,128)(2,1)S(1)} %broadcast_select_fusion) | copy-start | bytes 2359300
  64.1 0.9 copy-start.14
  64.1 1.2 copy-start.19
  65.4 0.9 copy-start.8
  65.4 0.9 copy-start.17
  67.9 131.1 %all-reduce.5.cloned.1.call-start = ((), (), s32[]{:S(2)}) async-start(), calls=%async_computation.5 | async-start | bytes 1048576 | tf_op jit(solution)/shard_map/psum | solution.py:95
  121.5 2.3 copy-start.12
  123.4 76.8 %copy-start.5 = (bf16[256,512]{1,0:T(8,128)(2,1)S(1)}, bf16[256,512]{1,0:T(8,128)(2,1)}, u32[]{:S(2)}) copy-start(bf16[256,512]{1,0:T(8,128)(2,1)} %param.14) | copy-start | bytes 786436
  124.9 156.8 %all-reduce.7.cloned.1.call-start = ((), (), s32[]{:S(2)}) async-start(), calls=%async_computation.6 | async-start | bytes 2097152 | tf_op jit(solution)/shard_map/psum | solution.py:106
  199.0 2.6 copy-start.2
  204.3 79.2 %copy-start.3 = (f32[96,512]{1,0:T(8,128)S(1)}, f32[96,512]{1,0:T(8,128)}, u32[]{:S(2)}) copy-start(f32[96,512]{1,0:T(8,128)} %reduce-scatter.5.cloned.1.call-done) | copy-start | bytes 589828
  204.4 187.2 %all-reduce.9.cloned.1.call-start = ((), (), s32[]{:S(2)}) async-start(), calls=%async_computation.7 | async-start | bytes 1572864 | tf_op jit(solution)/shard_map/psum | solution.py:146
  284.0 16.8 %copy-start.15 = (bf16[1536,64]{0,1:T(8,128)(2,1)S(1)}, bf16[1536,64]{0,1:T(8,128)(2,1)}, u32[]{:S(2)}) copy-start(bf16[1536,64]{0,1:T(8,128)(2,1)} %param.15) | copy-start | bytes 589828
  300.1 0.6 copy-start.13
  309.3 1.4 copy-start.4
  316.5 91.8 %copy-start.7 = (bf16[768,512]{1,0:T(8,128)(2,1)S(1)}, bf16[768,512]{1,0:T(8,128)(2,1)}, u32[]{:S(2)}) copy-start(bf16[768,512]{1,0:T(8,128)(2,1)} %copy-done.6) | copy-start | bytes 2359300
  316.6 91.8 %copy-start.9 = (bf16[768,512]{1,0:T(8,128)(2,1)S(1)}, bf16[768,512]{1,0:T(8,128)(2,1)}, u32[]{:S(2)}) copy-start(bf16[768,512]{1,0:T(8,128)(2,1)} %copy-done.8) | copy-start | bytes 2359300
  393.4 42.5 %all-to-all-start.1 = ((bf16[64,8,512]{2,1,0:T(8,128)(2,1)}), bf16[64,8,512]{2,1,0:T(8,128)(2,1)S(1)}, u32[]{:S(2)}, u32[]{:S(2)}) async-start(bf16[64,8,512]{2,1,0:T(8,128)(2,1)} %slice_bitcast_fusion), calls=%async_computation.2 | async-start | bytes 1048576 | tf_op jit(solution)/shard_map/all_to_all | solution.py:148
  408.3 3.9 copy-start.10
  408.3 597.0 %reduce-scatter.7.cloned.1.call-start = ((), (), s32[]{:S(2)}) async-start(), calls=%async_computation.8 | async-start | bytes 798720
Sparse Core Ops, SparseCore 0:
  68.0 33.9 reduce-scatter.4
  125.0 73.9 all-reduce.4
  204.5 77.1 all-reduce.6
  316.7 74.7 all-reduce.8
  413.8 591.4 reduce-scatter.6
where the time goes:
time: 1020 us; the launch traced here: 1010 us
  waiting for transfers between devices  873 us (86%)
  starting transfers between devices  34.2 us (3%)
  blocking collectives  31.4 us (3%)
  other arithmetic  24.8 us (2%)
  local copies, waits for them, and re-layouts  17.2 us (2%)
  matrix products  16.2 us (2%)
  between operations  14.9 us (1%)
    unnamed x6, waiting for transfers between devices  565 us
    psum x1, waiting for transfers between devices, per_device(): lax.psum(jnp.dot(d_preact_node, node_first.T, preferred_element_type=jnp....  77.1 us
    psum x1, waiting for transfers between devices, per_device(): lax.psum(combined.astype(jnp.bfloat16), 'hid').astype(jnp.float32)  75 us
    psum x1, waiting for transfers between devices, per_device(): lax.psum(jnp.dot(hidden_node, node_second, preferred_element_type=jnp.flo...  74.1 us
    reduce_scatter x1, waiting for transfers between devices, per_device(): lax.psum_scatter(jnp.dot(hidden, edge_second, preferred_element_type=jnp....  33.3 us
    all_to_all x1, waiting for transfers between devices, per_device(): lax.all_to_all(supply, 'tile', split_axis=0, concat_axis=0, tiled=True)  26.3 us
    all_to_all x1, waiting for transfers between devices, per_device(): lax.all_to_all(halo_part.astype(jnp.bfloat16), 'tile', split_axis=0, conc...  22.7 us
  transfers between devices with their start and end apart: 7, of which 7 were waited for; matrix products, arithmetic and copies ran while one was open for 1% of the time, Pallas kernels for 0%

commit v1 on v0

v1 whole, which is shorter than its diff:
```python
import jax
import jax.numpy as jnp
from jax import lax
from jax.experimental import pallas as pl
from jax.experimental.pallas import tpu as pltpu
from jax.sharding import Mesh, PartitionSpec as P

TILE = 128
epsilon = 1e-05
bf16 = jnp.bfloat16
f32 = jnp.float32
VMEM_LIMIT = 56 * 1024 * 1024
CHUNK = 32


def nn(a, b):
    return lax.dot_general(a, b, (((1,), (0,)), ((), ())), preferred_element_type=f32)


def nt(a, b):
    return lax.dot_general(a, b, (((1,), (1,)), ((), ())), preferred_element_type=f32)


def tn(a, b):
    return lax.dot_general(a, b, (((0,), (0,)), ((), ())), preferred_element_type=f32)


def onehot_rows(index_row, count):
    n = index_row.shape[1]
    column = jnp.broadcast_to(index_row, (TILE, n)).T
    lanes = lax.broadcasted_iota(jnp.int32, (n, TILE), 1)
    return jnp.concatenate(
        [(column == lanes + k * TILE).astype(f32).astype(bf16) for k in range(count // TILE)],
        axis=1,
    )


def onehot_columns(index_row, count):
    n = index_row.shape[1]
    rows = lax.broadcasted_iota(jnp.int32, (count, n), 0)
    return (index_row == rows).astype(f32).astype(bf16)


def supply_kernel(nodes, send, first, second, node_first, node_second, supply, weights):
    core = lax.axis_index("core")
    half = nodes.shape[1] // 2
    hot = onehot_rows(send[...], nodes.shape[0])
    columns = pl.ds(pl.multiple_of(core * half, half), half)
    supply[...] = nn(hot, nodes[:, columns]).astype(bf16)
    weights[...] = jnp.concatenate(
        [
            first[...].astype(f32).T.astype(bf16),
            node_first[...].astype(f32).T.astype(bf16),
            second[...],
            node_second[...],
        ],
        axis=1,
    )


def sigmoid(v):
    return 0.5 * jnp.tanh(0.5 * v) + 0.5


def normed(v):
    centre = jnp.mean(v, axis=-1, keepdims=True)
    shifted = v - centre
    variance = jnp.mean(shifted * shifted, axis=-1, keepdims=True)
    scale = lax.rsqrt(variance + epsilon)
    return shifted * scale, scale


def normed_back(g, unit, scale):
    return scale * (
        g
        - jnp.mean(g, axis=-1, keepdims=True)
        - unit * jnp.mean(g * unit, axis=-1, keepdims=True)
    )


def by_rows(total, body):
    def step(i, carry):
        body(pl.ds(pl.multiple_of(i * CHUNK, CHUNK), CHUNK))
        return carry

    lax.fori_loop(0, total // CHUNK, step, 0, unroll=2)


def step_kernel(
    tiles,
    live,
    nodes,
    edges,
    cotangent,
    halo,
    weights,
    sender,
    position,
    node_out,
    outgoing,
    base,
    table,
    stacked,
    wide,
    slope,
    unit,
    scale,
    low,
    received,
):
    d = nodes.shape[1]
    half = d // 2
    n = nodes.shape[0]
    e = edges.shape[0]
    h = halo.shape[0] // 2
    core = lax.axis_index("core")
    share = 2 * lax.axis_index("y") + core
    first = weights.at[:, : 3 * d]
    node_first = weights.at[:, 3 * d : 5 * d]
    second = weights.at[:, 5 * d : 6 * d]
    node_second = weights.at[:, 6 * d : 7 * d]

    table[:n] = nodes[...]
    table[n:, :half] = halo[:h]
    table[n:, half:] = halo[h:]
    receiver = jnp.concatenate(
        [
            jnp.where(
                b < live[0], position[:, b * TILE : (b + 1) * TILE] + tiles[b] * TILE, -1
            )
            for b in range(e // TILE)
        ],
        axis=1,
    )
    received[...] = onehot_rows(receiver, n)
    stacked[:, :d] = edges[...]
    stacked[:, d : 2 * d] = nn(onehot_rows(sender[...], n + h), table[...]).astype(bf16)
    stacked[:, 2 * d :] = nn(received[...], nodes[...]).astype(bf16)

    wide[...] = nt(stacked[...], first[...])

    def activate(rows):
        v = wide[rows, :]
        s = sigmoid(v)
        low[rows, :] = (v * s).astype(bf16)
        slope[rows, :] = s * (1.0 + v * (1.0 - s))

    by_rows(e, activate)
    wide[...] = nn(low[...], second[...])

    def normalise(rows):
        u, r = normed(wide[rows, :])
        unit[rows, :] = u
        scale[rows, :] = jnp.broadcast_to(r, (CHUNK, TILE))
        low[rows, :] = (edges[rows, :].astype(f32) + u).astype(bf16)

    by_rows(e, normalise)
    back = onehot_columns(receiver, n)
    aggregated = nn(back, low[...]).astype(bf16)

    preact_node = nt(jnp.concatenate([nodes[...], aggregated], axis=1), node_first[...])
    s = sigmoid(preact_node)
    hidden_node = (preact_node * s).astype(bf16)
    node_unit, node_scale = normed(nn(hidden_node, node_second[...]))
    node_out[...] = (nodes[...].astype(f32) + node_unit).astype(bf16)
    d_node_sum = normed_back(cotangent[...].astype(f32), node_unit, node_scale).astype(bf16)
    d_preact_node = (
        nt(d_node_sum, node_second[...]) * (s * (1.0 + preact_node * (1.0 - s)))
    ).astype(bf16)
    d_aggregated = nn(d_preact_node, node_first[:, d:]).astype(bf16)
    columns = pl.ds(pl.multiple_of(core * half, half), half)
    base[...] = cotangent[:, columns].astype(f32) + nn(
        d_preact_node, weights[:, pl.ds(pl.multiple_of(3 * d + core * half, half), half)]
    )

    wide[...] = nn(received[...], d_aggregated)

    def denormalise(rows):
        low[rows, :] = normed_back(wide[rows, :], unit[rows, :], scale[rows, :1]).astype(bf16)

    by_rows(e, denormalise)
    wide[...] = nt(low[...], second[...])

    def deactivate(rows):
        low[rows, :] = (wide[rows, :] * slope[rows, :]).astype(bf16)

    by_rows(e, deactivate)

    units = weights.shape[0]
    own = units // 8
    pick = (
        lax.broadcasted_iota(jnp.int32, (units, own), 0)
        == lax.broadcasted_iota(jnp.int32, (units, own), 1) + share * own
    )
    d_own = nn(low[...], pick.astype(f32).astype(bf16))
    grad = tn(d_own.astype(bf16), stacked[...]).T.reshape(64, 3 * d // 64, own)
    left = grad[:, :16]
    right = jnp.concatenate([grad[:, 16:], jnp.zeros((64, 8, own), f32)], axis=1)
    packed = jnp.concatenate([left, right], axis=2)

    d_sender = nn(
        low[...], weights[:, pl.ds(pl.multiple_of(d + core * half, half), half)]
    ).astype(bf16)
    d_receiver = nn(
        low[...], weights[:, pl.ds(pl.multiple_of(2 * d + core * half, half), half)]
    ).astype(bf16)
    table_grad = nn(onehot_columns(sender[...], n + h), d_sender)
    base[...] += table_grad[:n] + nn(back, d_receiver)
    outgoing[...] = jnp.concatenate(
        [
            table_grad[n:, :TILE].reshape(64, 8, TILE),
            table_grad[n:, TILE:].reshape(64, 8, TILE),
            packed,
        ],
        axis=1,
    ).astype(bf16)


def finish_kernel(incoming, base, send, node_grad, first_grad):
    values = incoming[...].astype(f32)
    rows = values.shape[0] * 8
    returned = jnp.concatenate(
        [values[:, :8].reshape(rows, TILE), values[:, 8:16].reshape(rows, TILE)], axis=1
    ).astype(bf16)
    hot = onehot_columns(send[...], base.shape[0])
    node_grad[...] = (base[...] + nn(hot, returned)).astype(bf16)
    total = jnp.sum(values[:, 16:], axis=0)
    own = first_grad.shape[1]
    first_grad[...] = jnp.concatenate([total[:, :own], total[:8, own:]], axis=0)


def per_device(
    nodes,
    edges,
    node_cotangent,
    edge_first,
    edge_second,
    node_first,
    node_second,
    sender,
    receiver_pos,
    block_tile,
    live_blocks,
    send_rows,
):
    n, d = nodes.shape
    e = edges.shape[0]
    half = d // 2
    peers, slots = send_rows.shape[1], send_rows.shape[2]
    h = peers * slots
    shares = lax.axis_size(("y", "core"))
    units = edge_second.shape[0] * shares
    own = edge_second.shape[0]
    width = edge_first.shape[0] + node_first.shape[0] + 2 * d
    vmem = pl.BlockSpec(memory_space=pltpu.VMEM)
    smem = pl.BlockSpec(memory_space=pltpu.SMEM)
    params = pltpu.CompilerParams(vmem_limit_bytes=VMEM_LIMIT)
    send = send_rows.reshape(1, h)

    supply, share = pl.pallas_call(
        supply_kernel,
        out_shape=(
            jax.ShapeDtypeStruct((h, half), bf16),
            jax.ShapeDtypeStruct((own, width), bf16),
        ),
        in_specs=[vmem] * 6,
        out_specs=(vmem, vmem),
        compiler_params=params,
        name="supply",
    )(nodes, send, edge_first, edge_second, node_first, node_second)
    weights = lax.all_gather(share, ("y", "core"), axis=0, tiled=True)
    received = lax.all_to_all(
        supply.reshape(peers, slots, half), ("x", "z"), split_axis=0, concat_axis=0, tiled=True
    ).reshape(h, half)
    halo = lax.all_gather(received, "core", axis=0, tiled=True)

    node_out, outgoing, base = pl.pallas_call(
        step_kernel,
        out_shape=(
            jax.ShapeDtypeStruct((n, d), bf16),
            jax.ShapeDtypeStruct((peers, 32, TILE), bf16),
            jax.ShapeDtypeStruct((n, half), f32),
        ),
        in_specs=[smem, smem] + [vmem] * 7,
        out_specs=(vmem, vmem, vmem),
        scratch_shapes=[
            pltpu.VMEM((n + h, d), bf16),
            pltpu.VMEM((e, 3 * d), bf16),
            pltpu.VMEM((e, units), f32),
            pltpu.VMEM((e, units), f32),
            pltpu.VMEM((e, d), f32),
            pltpu.VMEM((e, TILE), f32),
            pltpu.VMEM((e, units), bf16),
            pltpu.VMEM((e, n), bf16),
        ],
        compiler_params=params,
        name="step",
    )(
        block_tile,
        live_blocks,
        nodes,
        edges,
        node_cotangent,
        halo,
        weights,
        sender.reshape(1, e),
        receiver_pos.reshape(1, e),
    )
    incoming = lax.all_to_all(outgoing, ("x", "z"), split_axis=0, concat_axis=0, tiled=True)
    half_grad, first_grad = pl.pallas_call(
        finish_kernel,
        out_shape=(
            jax.ShapeDtypeStruct((n, half), bf16),
            jax.ShapeDtypeStruct((edge_first.shape[0] // peers, own), f32),
        ),
        in_specs=[vmem] * 3,
        out_specs=(vmem, vmem),
        compiler_params=params,
        name="finish",
    )(incoming, base, send)
    node_grad = lax.all_gather(half_grad, "core", axis=1, tiled=True)
    return (node_out, node_grad, first_grad)


def solution(mesh):
    devices = mesh.devices
    tiles, shares = devices.shape
    fine = Mesh(devices.reshape(4, tiles // 4, shares // 2, 2), ("x", "z", "y", "core"))
    tile = ("x", "z")
    hid = ("y", "core")
    in_specs = (
        P(tile, None),
        P(tile, None),
        P(tile, None),
        P(None, hid),
        P(hid, None),
        P(None, hid),
        P(hid, None),
        P(tile),
        P(tile),
        P(tile),
        P(tile),
        P(tile, None, None),
    )
    out_specs = (P(tile, None), P(tile, None), P(tile, hid))
    return jax.shard_map(
        per_device, mesh=fine, in_specs=in_specs, out_specs=out_specs, check_vma=False
    )
```

time: 1020 us -> 135 us (0.13)
  waiting for transfers between devices: 873 us -> 16.2 us
  other arithmetic: 24.8 us -> 0 us
  blocking collectives: 31.4 us -> 55.2 us
  Pallas kernels: 0 us -> 20.6 us
  matrix products: 16.2 us -> 0 us
  starting transfers between devices: 34.2 us -> 19.2 us
    unnamed x6 -> x1, waiting for transfers between devices: 565 us -> 0.02 us
    psum x3 -> x0, waiting for transfers between devices: 226 us -> none  [the longest x1 77.1 us: per_device(): lax.psum(jnp.dot(d_preact_node, node_first.T, preferred_element_type=jnp....]
    all_to_all x0 -> x1, blocking collectives: none -> 45.5 us  [per_device(): lax.all_to_all(outgoing, ('x', 'z'), split_axis=0, concat_axis=0, tiled=T...]
    reduce_scatter x1 -> x0, waiting for transfers between devices: 33.3 us -> none  [per_device(): lax.psum_scatter(jnp.dot(hidden, edge_second, preferred_element_type=jnp....]
    all_to_all x2 -> x1, waiting for transfers between devices: 49 us -> 15.8 us  [per_device(): lax.all_to_all(supply.reshape(peers, slots, half), ('x', 'z'), split_axis...]
    all_gather x2, blocking collectives: 31.4 us -> 9.75 us  [the longest x1 4.98 us: per_device(): halo = lax.all_gather(received, 'core', axis=0, tiled=True)]
    pallas_call x0 -> x3, Pallas kernels: none -> 20.6 us  [the longest x1 16.2 us: per_device(): pl.pallas_call(step_kernel, out_shape=(jax.ShapeDtypeStruct((n, d), bf16)...]
    dot_general x14 -> x0, matrix products: 16.2 us -> none  [the longest x3 5.78 us: tile_sum(): jnp.einsum('bt,bpd->tpd', tile_hot, per_block, precision=lax.Precision.HI...]
  transfers between devices with their start and end apart: 7 -> 2, of which waited for: 7 -> 2; matrix products, arithmetic and copies ran while one was open for 1% -> 2% of each run, Pallas kernels for 0% -> 0%
where the time goes in v1:
time: 135 us; the launch traced here: 134 us
  blocking collectives  55.2 us (41%)
  Pallas kernels  20.6 us (15%)
  starting transfers between devices  19.2 us (14%)
  waiting for transfers between devices  16.2 us (12%)
  between operations  14.7 us (11%)
  local copies, waits for them, and re-layouts  8.3 us (6%)
    all_to_all x1, blocking collectives, per_device(): lax.all_to_all(outgoing, ('x', 'z'), split_axis=0, concat_axis=0, tiled=T...  45.5 us
    all_to_all x1, starting transfers between devices, per_device(): lax.all_to_all(supply.reshape(peers, slots, half), ('x', 'z'), split_axis...  19.1 us
    pallas_call x1, Pallas kernels, per_device(): pl.pallas_call(step_kernel, out_shape=(jax.ShapeDtypeStruct((n, d), bf16)...  16.2 us
    all_to_all x1, waiting for transfers between devices, per_device(): lax.all_to_all(supply.reshape(peers, slots, half), ('x', 'z'), split_axis...  15.8 us
    unnamed x4, local copies, waits for them, and re-layouts  5.06 us
    all_gather x1, blocking collectives, per_device(): halo = lax.all_gather(received, 'core', axis=0, tiled=True)  4.98 us
    all_gather x1, blocking collectives, per_device(): node_grad = lax.all_gather(half_grad, 'core', axis=1, tiled=True)  4.77 us
  transfers between devices with their start and end apart: 2, of which 2 were waited for; matrix products, arithmetic and copies ran while one was open for 2% of the time, Pallas kernels for 0%

profile of v1, /device:TPU:1, one launch (start us, length us, event | category | flops | bytes accessed | tf_op | source)
XLA Modules:
  0.0 134.1 jit_solution(5695929365092906948)
XLA Ops:
  7.2 0.0 all-gather.2.cloned.1.call-start
  7.2 0.8 copy.18
  8.0 0.7 reshape.21.send
  8.7 1.7 %copy.20.node_first = bf16[1024,64]{1,0:T(8,128)(2,1)} copy(bf16[1024,64]{0,1:T(8,128)(2,1)} %param.17) | data formatting | bytes 262144 | tf_op args[5]
  10.4 1.8 %copy.19.first = bf16[1536,64]{1,0:T(8,128)(2,1)} copy(bf16[1536,64]{0,1:T(8,128)(2,1)} %param.15) | data formatting | bytes 393216 | tf_op args[3]
  12.3 2.4 %supply.1 = (bf16[512,256]{1,0:T(8,128)(2,1)}, bf16[64,3584]{1,0:T(8,128)(2,1)}) custom-call(bf16[256,512]{1,0:T(8,128)(2,1)} %nodes.3, s32[1,512]{1,0:T(1,128)} %reshape.21.send, bf16[1536,64]{1,0:T(8,128)(2,1)} %copy.19.first, bf16[64,512]{1,0:T(8,128)(2,1)} %second.1, bf16[1024,64]{1,0:T(8,128)(2,1)} %copy.20.node_first, bf16[64,512]{1,0:T(8,128)(2,1)} %node_second.1), custom_call_target="tpu_custom_call" | custom-call | tf_op jit(solution)/shard_map/supply/pallas_call | solution.py:260
  14.6 0.0 all-gather.2.cloned.1.call-update
  14.6 19.1 %all-to-all-start = ((bf16[64,8,256]{2,1,0:T(8,128)(2,1)}), bf16[64,8,256]{2,1,0:T(8,128)(2,1)S(1)}, u32[]{:S(2)}, u32[]{:S(2)}) async-start(bf16[64,8,256]{2,1,0:T(8,128)(2,1)} %bitcast.3), calls=%async_computation | async-start | bytes 524288 | tf_op jit(solution)/shard_map/all_to_all | solution.py:272
  34.4 1.3 reshape.24.sender
  35.7 1.3 reshape.25.position
  37.0 15.8 %all-to-all-done = bf16[64,8,256]{2,1,0:T(8,128)(2,1)S(1)} async-done(((bf16[64,8,256]{2,1,0:T(8,128)(2,1)}), bf16[64,8,256]{2,1,0:T(8,128)(2,1)S(1)}, u32[]{:S(2)}, u32[]{:S(2)}) %all-to-all-start) | async-done | bytes 262176 | tf_op jit(solution)/shard_map/all_to_all | solution.py:272
  52.8 5.0 %all_gather.9.halo = bf16[1024,256]{1,0:T(8,128)(2,1)} all-gather(bf16[512,256]{1,0:T(8,128)(2,1)S(1)} %bitcast.2), channel_id=1, replica_groups=mesh['x'=4,'z'=16,'y'=4,'core'=2] {'core'}, dimensions={0}, use_global_device_ids=true | all-gather | bytes 786432 | tf_op jit(solution)/shard_map/all_gather | solution.py:275
  57.8 0.3 all-gather.2.cloned.1.call-done.weights
  58.1 16.2 %step.1 = (bf16[256,512]{1,0:T(8,128)(2,1)}, bf16[64,32,128]{2,1,0:T(8,128)(2,1)}, f32[256,256]{1,0:T(8,128)}) custom-call(s32[6]{0:T(128)} %tiles.1, s32[1]{0:T(128)S(6)} %copy.22.live, bf16[256,512]{1,0:T(8,128)(2,1)} %nodes.3, bf16[768,512]{1,0:T(8,128)(2,1)} %edges.1, bf16[256,512]{1,0:T(8,128)(2,1)} %cotangent.1, bf16[1024,256]{1,0:T(8,128)(2,1)} %all_gather.9.halo, ...), custom_call_target="tpu_custom_call" | custom-call | tf_op jit(solution)/shard_map/step/pallas_call | solution.py:277
  74.4 45.5 %all_to_all.10.incoming = bf16[64,32,128]{2,1,0:T(8,128)(2,1)} all-to-all(bf16[64,32,128]{2,1,0:T(8,128)(2,1)} %get-tuple-element.13), channel_id=1, replica_groups=mesh['x'=4,'z'=16,'y'=4,'core'=2] {'x','z'}, dimensions={0} | all-to-all | bytes 1048576 | tf_op jit(solution)/shard_map/all_to_all | solution.py:309
  119.8 2.0 %finish.1 = (bf16[256,256]{1,0:T(8,128)(2,1)}, f32[24,64]{1,0:T(8,128)}) custom-call(bf16[64,32,128]{2,1,0:T(8,128)(2,1)} %all_to_all.10.incoming, f32[256,256]{1,0:T(8,128)} %get-tuple-element.14.base, s32[1,512]{1,0:T(1,128)} %reshape.21.send), custom_call_target="tpu_custom_call" | custom-call | tf_op jit(solution)/shard_map/finish/pallas_call | solution.py:310
  121.8 4.8 %all_gather.11 = bf16[256,512]{1,0:T(8,128)(2,1)S(1)} all-gather(bf16[256,256]{1,0:T(8,128)(2,1)} %get-tuple-element.15), channel_id=1, replica_groups=mesh['x'=4,'z'=16,'y'=4,'core'=2] {'core'}, dimensions={1}, use_global_device_ids=true | all-gather | bytes 393216 | tf_op jit(solution)/shard_map/all_gather | solution.py:321
  126.6 0.7 copy.23
Async XLA Ops:
  7.2 51.0 %all-gather.2.cloned.1.call-start = ((), (), s32[]{:S(2)}) async-start(), calls=%async_computation.2 | async-start | bytes 4128768 | tf_op jit(solution)/shard_map/all_gather | solution.py:271
  14.6 38.2 %all-to-all-start = ((bf16[64,8,256]{2,1,0:T(8,128)(2,1)}), bf16[64,8,256]{2,1,0:T(8,128)(2,1)S(1)}, u32[]{:S(2)}, u32[]{:S(2)}) async-start(bf16[64,8,256]{2,1,0:T(8,128)(2,1)} %bitcast.3), calls=%async_computation | async-start | bytes 524288 | tf_op jit(solution)/shard_map/all_to_all | solution.py:272
Sparse Core Ops, SparseCore 0:
  14.8 43.3 all-gather.1

commit v2 on v1

--- a/solution.py
+++ b/solution.py
@@ -41,21 +41,28 @@
     return (index_row == rows).astype(f32).astype(bf16)
 
 
+def flat_row(rows):
+    return jnp.concatenate([rows[i : i + 1] for i in range(rows.shape[0])], axis=1)
+
+
+def slot_order(slots, peers):
+    count = slots * peers
+    row = lax.broadcasted_iota(jnp.int32, (count, count), 0)
+    column = lax.broadcasted_iota(jnp.int32, (count, count), 1)
+    return ((row % slots) * peers + row // slots == column).astype(f32).astype(bf16)
+
+
 def supply_kernel(nodes, send, first, second, node_first, node_second, supply, weights):
     core = lax.axis_index("core")
     half = nodes.shape[1] // 2
-    hot = onehot_rows(send[...], nodes.shape[0])
+    hot = onehot_rows(flat_row(send[...]), nodes.shape[0])
     columns = pl.ds(pl.multiple_of(core * half, half), half)
-    supply[...] = nn(hot, nodes[:, columns]).astype(bf16)
-    weights[...] = jnp.concatenate(
-        [
-            first[...].astype(f32).T.astype(bf16),
-            node_first[...].astype(f32).T.astype(bf16),
-            second[...],
-            node_second[...],
-        ],
-        axis=1,
-    )
+    rows = nn(hot, nodes[:, columns]).astype(bf16)
+    supply[...] = nn(slot_order(*send.shape), rows).astype(bf16)
+    at = 0
+    for part in (first, node_first, second, node_second):
+        weights[:, at : at + part.shape[1]] = part[...]
+        at += part.shape[1]
 
 
 def sigmoid(v):
@@ -93,7 +100,11 @@
     edges,
     cotangent,
     halo,
-    weights,
+    pair,
+    near,
+    far,
+    near_other,
+    far_other,
     sender,
     position,
     node_out,
@@ -107,6 +118,7 @@
     scale,
     low,
     received,
+    weights,
 ):
     d = nodes.shape[1]
     half = d // 2
@@ -114,11 +126,21 @@
     e = edges.shape[0]
     h = halo.shape[0] // 2
     core = lax.axis_index("core")
-    share = 2 * lax.axis_index("y") + core
-    first = weights.at[:, : 3 * d]
-    node_first = weights.at[:, 3 * d : 5 * d]
-    second = weights.at[:, 5 * d : 6 * d]
-    node_second = weights.at[:, 6 * d : 7 * d]
+    first = pl.ds(0, 3 * d)
+    node_first = pl.ds(3 * d, 2 * d)
+    second = pl.ds(5 * d, d)
+    node_second = pl.ds(6 * d, d)
+    parts = (pair, near, far, near_other, far_other)
+    units = 0
+    for piece in parts:
+        weights[units : units + piece.shape[0], :] = piece[...]
+        units += piece.shape[0]
+
+    def to_units(x, columns):
+        return nt(x, weights[:, columns])
+
+    def from_units(x, columns):
+        return nn(x, weights[:, columns])
 
     table[:n] = nodes[...]
     table[n:, :half] = halo[:h]
@@ -126,18 +148,19 @@
     receiver = jnp.concatenate(
         [
             jnp.where(
-                b < live[0], position[:, b * TILE : (b + 1) * TILE] + tiles[b] * TILE, -1
+                b < live[0], position[b : b + 1, :] + tiles[b] * TILE, -1
             )
             for b in range(e // TILE)
         ],
         axis=1,
     )
     received[...] = onehot_rows(receiver, n)
+    senders = flat_row(sender[...])
     stacked[:, :d] = edges[...]
-    stacked[:, d : 2 * d] = nn(onehot_rows(sender[...], n + h), table[...]).astype(bf16)
+    stacked[:, d : 2 * d] = nn(onehot_rows(senders, n + h), table[...]).astype(bf16)
     stacked[:, 2 * d :] = nn(received[...], nodes[...]).astype(bf16)
 
-    wide[...] = nt(stacked[...], first[...])
+    wide[...] = to_units(stacked[...], first)
 
     def activate(rows):
         v = wide[rows, :]
@@ -146,7 +169,7 @@
         slope[rows, :] = s * (1.0 + v * (1.0 - s))
 
     by_rows(e, activate)
-    wide[...] = nn(low[...], second[...])
+    wide[...] = from_units(low[...], second)
 
     def normalise(rows):
         u, r = normed(wide[rows, :])
@@ -158,19 +181,19 @@
     back = onehot_columns(receiver, n)
     aggregated = nn(back, low[...]).astype(bf16)
 
-    preact_node = nt(jnp.concatenate([nodes[...], aggregated], axis=1), node_first[...])
+    preact_node = to_units(jnp.concatenate([nodes[...], aggregated], axis=1), node_first)
     s = sigmoid(preact_node)
     hidden_node = (preact_node * s).astype(bf16)
-    node_unit, node_scale = normed(nn(hidden_node, node_second[...]))
+    node_unit, node_scale = normed(from_units(hidden_node, node_second))
     node_out[...] = (nodes[...].astype(f32) + node_unit).astype(bf16)
     d_node_sum = normed_back(cotangent[...].astype(f32), node_unit, node_scale).astype(bf16)
     d_preact_node = (
-        nt(d_node_sum, node_second[...]) * (s * (1.0 + preact_node * (1.0 - s)))
-    ).astype(bf16)
-    d_aggregated = nn(d_preact_node, node_first[:, d:]).astype(bf16)
+        to_units(d_node_sum, node_second) * (s * (1.0 + preact_node * (1.0 - s)))
+    ).astype(bf16)
+    d_aggregated = from_units(d_preact_node, pl.ds(4 * d, d)).astype(bf16)
     columns = pl.ds(pl.multiple_of(core * half, half), half)
-    base[...] = cotangent[:, columns].astype(f32) + nn(
-        d_preact_node, weights[:, pl.ds(pl.multiple_of(3 * d + core * half, half), half)]
+    base[...] = cotangent[:, columns].astype(f32) + from_units(
+        d_preact_node, pl.ds(pl.multiple_of(3 * d + core * half, half), half)
     )
 
     wide[...] = nn(received[...], d_aggregated)
@@ -179,18 +202,17 @@
         low[rows, :] = normed_back(wide[rows, :], unit[rows, :], scale[rows, :1]).astype(bf16)
 
     by_rows(e, denormalise)
-    wide[...] = nt(low[...], second[...])
+    wide[...] = to_units(low[...], second)
 
     def deactivate(rows):
         low[rows, :] = (wide[rows, :] * slope[rows, :]).astype(bf16)
 
     by_rows(e, deactivate)
 
-    units = weights.shape[0]
     own = units // 8
     pick = (
         lax.broadcasted_iota(jnp.int32, (units, own), 0)
-        == lax.broadcasted_iota(jnp.int32, (units, own), 1) + share * own
+        == lax.broadcasted_iota(jnp.int32, (units, own), 1) + core * own
     )
     d_own = nn(low[...], pick.astype(f32).astype(bf16))
     grad = tn(d_own.astype(bf16), stacked[...]).T.reshape(64, 3 * d // 64, own)
@@ -198,13 +220,13 @@
     right = jnp.concatenate([grad[:, 16:], jnp.zeros((64, 8, own), f32)], axis=1)
     packed = jnp.concatenate([left, right], axis=2)
 
-    d_sender = nn(
-        low[...], weights[:, pl.ds(pl.multiple_of(d + core * half, half), half)]
-    ).astype(bf16)
-    d_receiver = nn(
-        low[...], weights[:, pl.ds(pl.multiple_of(2 * d + core * half, half), half)]
-    ).astype(bf16)
-    table_grad = nn(onehot_columns(sender[...], n + h), d_sender)
+    d_sender = from_units(
+        low[...], pl.ds(pl.multiple_of(d + core * half, half), half)
+    ).astype(bf16)
+    d_receiver = from_units(
+        low[...], pl.ds(pl.multiple_of(2 * d + core * half, half), half)
+    ).astype(bf16)
+    table_grad = nn(onehot_columns(senders, n + h), d_sender)
     base[...] += table_grad[:n] + nn(back, d_receiver)
     outgoing[...] = jnp.concatenate(
         [
@@ -222,8 +244,9 @@
     returned = jnp.concatenate(
         [values[:, :8].reshape(rows, TILE), values[:, 8:16].reshape(rows, TILE)], axis=1
     ).astype(bf16)
-    hot = onehot_columns(send[...], base.shape[0])
-    node_grad[...] = (base[...] + nn(hot, returned)).astype(bf16)
+    hot = onehot_columns(flat_row(send[...]), base.shape[0])
+    by_slot = tn(slot_order(*send.shape), returned).astype(bf16)
+    node_grad[...] = (base[...] + nn(hot, by_slot)).astype(bf16)
     total = jnp.sum(values[:, 16:], axis=0)
     own = first_grad.shape[1]
     first_grad[...] = jnp.concatenate([total[:, :own], total[:8, own:]], axis=0)
@@ -248,16 +271,16 @@
     half = d // 2
     peers, slots = send_rows.shape[1], send_rows.shape[2]
     h = peers * slots
-    shares = lax.axis_size(("y", "core"))
-    units = edge_second.shape[0] * shares
+    columns = lax.axis_size("y")
     own = edge_second.shape[0]
+    units = own * columns * lax.axis_size("core")
     width = edge_first.shape[0] + node_first.shape[0] + 2 * d
     vmem = pl.BlockSpec(memory_space=pltpu.VMEM)
     smem = pl.BlockSpec(memory_space=pltpu.SMEM)
     params = pltpu.CompilerParams(vmem_limit_bytes=VMEM_LIMIT)
-    send = send_rows.reshape(1, h)
-
-    supply, share = pl.pallas_call(
+    send = send_rows[0].T
+
+    supply, shard = pl.pallas_call(
         supply_kernel,
         out_shape=(
             jax.ShapeDtypeStruct((h, half), bf16),
@@ -267,11 +290,22 @@
         out_specs=(vmem, vmem),
         compiler_params=params,
         name="supply",
-    )(nodes, send, edge_first, edge_second, node_first, node_second)
-    weights = lax.all_gather(share, ("y", "core"), axis=0, tiled=True)
+    )(nodes, send, edge_first.T, edge_second, node_first.T, node_second)
+    pair = lax.all_gather(shard, "core", axis=0, tiled=True)
+    beside = [
+        (2 * i + c, 2 * ((i + (1, columns - 1)[c]) % columns) + c)
+        for i in range(columns)
+        for c in range(2)
+    ]
+    near = lax.ppermute(pair, ("y", "core"), beside)
+    start = lax.axis_index("core") * own
+    relayed = lax.dynamic_slice_in_dim(near, start, own, 0)
+    far = lax.ppermute(relayed, ("y", "core"), beside)
     received = lax.all_to_all(
         supply.reshape(peers, slots, half), ("x", "z"), split_axis=0, concat_axis=0, tiled=True
     ).reshape(h, half)
+    near_other = lax.ppermute(near, "core", [(0, 1), (1, 0)])
+    far_other = lax.ppermute(far, "core", [(0, 1), (1, 0)])
     halo = lax.all_gather(received, "core", axis=0, tiled=True)
 
     node_out, outgoing, base = pl.pallas_call(
@@ -281,7 +315,7 @@
             jax.ShapeDtypeStruct((peers, 32, TILE), bf16),
             jax.ShapeDtypeStruct((n, half), f32),
         ),
-        in_specs=[smem, smem] + [vmem] * 7,
+        in_specs=[smem, smem] + [vmem] * 11,
         out_specs=(vmem, vmem, vmem),
         scratch_shapes=[
             pltpu.VMEM((n + h, d), bf16),
@@ -292,6 +326,7 @@
             pltpu.VMEM((e, TILE), f32),
             pltpu.VMEM((e, units), bf16),
             pltpu.VMEM((e, n), bf16),
+            pltpu.VMEM((units, width), bf16),
         ],
         compiler_params=params,
         name="step",
@@ -302,9 +337,13 @@
         edges,
         node_cotangent,
         halo,
-        weights,
-        sender.reshape(1, e),
-        receiver_pos.reshape(1, e),
+        pair,
+        near,
+        far,
+        near_other,
+        far_other,
+        sender.reshape(e // TILE, TILE),
+        receiver_pos.reshape(e // TILE, TILE),
     )
     incoming = lax.all_to_all(outgoing, ("x", "z"), split_axis=0, concat_axis=0, tiled=True)
     half_grad, first_grad = pl.pallas_call(

time: 135 us -> 116 us (0.86)
  between operations: 14.7 us -> 1.38 us
  starting transfers between devices: 19.2 us -> 25.9 us
  local copies, waits for them, and re-layouts: 8.3 us -> 1.67 us
  waiting for transfers between devices: 16.2 us -> 11.8 us
    ppermute x0 -> x4, starting transfers between devices: none -> 10.3 us  [the longest x1 3.46 us: per_device(): far_other = lax.ppermute(far, 'core', [(0, 1), (1, 0)])]
    all_gather x0 -> x1, blocking collectives: none -> 9.17 us  [per_device(): pair = lax.all_gather(shard, 'core', axis=0, tiled=True)]
    all_to_all x1, waiting for transfers between devices: 15.8 us -> 7.2 us  [per_device(): lax.all_to_all(supply.reshape(peers, slots, half), ('x', 'z'), split_axis...]
    all_to_all x1, blocking collectives: 45.5 us -> 37.9 us  [per_device(): lax.all_to_all(outgoing, ('x', 'z'), split_axis=0, concat_axis=0, tiled=T...]
    ppermute x0 -> x4, waiting for transfers between devices: none -> 4.62 us  [the longest x1 4.61 us: per_device(): far = lax.ppermute(relayed, ('y', 'core'), beside)]
    all_to_all x1, starting transfers between devices: 19.1 us -> 15.6 us  [per_device(): lax.all_to_all(supply.reshape(peers, slots, half), ('x', 'z'), split_axis...]
    unnamed x4 -> x9, local copies, waits for them, and re-layouts: 5.06 us -> 1.63 us
    reshape x3 -> x0, local copies, waits for them, and re-layouts: 3.24 us -> none  [the longest x1 1.29 us: per_device(): receiver_pos.reshape(1, e)]
  transfers between devices with their start and end apart: 2 -> 5, of which waited for: 2 -> 2; matrix products, arithmetic and copies ran while one was open for 2% -> 0% of each run, Pallas kernels for 0% -> 0%
where the time goes in v2:
time: 116 us
  blocking collectives  54 us (47%)
  starting transfers between devices  25.9 us (22%)
  Pallas kernels  21.2 us (18%)
  waiting for transfers between devices  11.8 us (10%)
  local copies, waits for them, and re-layouts  1.67 us (1%)
  between operations  1.38 us (1%)
    all_to_all x1, blocking collectives, per_device(): lax.all_to_all(outgoing, ('x', 'z'), split_axis=0, concat_axis=0, tiled=T...  37.9 us
    pallas_call x1, Pallas kernels, per_device(): pl.pallas_call(step_kernel, out_shape=(jax.ShapeDtypeStruct((n, d), bf16)...  16.3 us
    all_to_all x1, starting transfers between devices, per_device(): lax.all_to_all(supply.reshape(peers, slots, half), ('x', 'z'), split_axis...  15.6 us
    all_gather x1, blocking collectives, per_device(): pair = lax.all_gather(shard, 'core', axis=0, tiled=True)  9.17 us
    all_to_all x1, waiting for transfers between devices, per_device(): lax.all_to_all(supply.reshape(peers, slots, half), ('x', 'z'), split_axis...  7.2 us
    all_gather x1, blocking collectives, per_device(): node_grad = lax.all_gather(half_grad, 'core', axis=1, tiled=True)  4.65 us
    ppermute x1, waiting for transfers between devices, per_device(): far = lax.ppermute(relayed, ('y', 'core'), beside)  4.61 us
    ppermute x1, starting transfers between devices, per_device(): far_other = lax.ppermute(far, 'core', [(0, 1), (1, 0)])  3.46 us
  transfers between devices with their start and end apart: 5, of which 2 were waited for; matrix products, arithmetic and copies ran while one was open for 0% of the time, Pallas kernels for 0%

profile of v2, /device:TPU:1, one launch (start us, length us, event | category | flops | bytes accessed | tf_op | source)
XLA Modules:
  0.0 116.0 jit_solution(17829553479926149259)
XLA Ops:
  0.6 2.6 %supply.1 = (bf16[512,256]{1,0:T(8,128)(2,1)}, bf16[64,3584]{1,0:T(8,128)(2,1)}) custom-call(bf16[256,512]{1,0:T(8,128)(2,1)} %nodes.3, s32[8,64]{1,0:T(8,128)} %bitcast.12, bf16[64,1536]{1,0:T(8,128)(2,1)} %bitcast.10, bf16[64,512]{1,0:T(8,128)(2,1)} %second.1, bf16[64,1024]{1,0:T(8,128)(2,1)} %bitcast.11, bf16[64,512]{1,0:T(8,128)(2,1)} %node_second.1), custom_call_target="tpu_custom_call" | custom-call | tf_op jit(solution)/shard_map/supply/pallas_call | solution.py:283
  3.3 9.2 %all_gather.10.pair = bf16[128,3584]{1,0:T(8,128)(2,1)S(1)} all-gather(bf16[64,3584]{1,0:T(8,128)(2,1)} %get-tuple-element.11), channel_id=1, replica_groups=mesh['x'=4,'z'=16,'y'=4,'core'=2] {'core'}, dimensions={0}, use_global_device_ids=true | all-gather | bytes 1376256 | tf_op jit(solution)/shard_map/all_gather | solution.py:294
  12.4 0.0 copy-start
  12.4 1.9 %collective-permute-start = (bf16[128,3584]{1,0:T(8,128)(2,1)S(1)}, bf16[128,3584]{1,0:T(8,128)(2,1)S(1)}, u32[]{:S(2)}, u32[]{:S(2)}) collective-permute-start(bf16[128,3584]{1,0:T(8,128)(2,1)S(1)} %all_gather.10.pair), channel_id=1, source_target_pairs={{0,2},{1,7},{2,4},{3,1},{4,6},{5,3},{6,0},{7,5},{8,10},{9,15},{10,... | collective-permute-start | bytes 2752520 | tf_op jit(solution)/shard_map/ppermute | solution.py:300
  14.3 15.6 %all-to-all-start = ((bf16[64,8,256]{2,1,0:T(8,128)(2,1)}), bf16[64,8,256]{2,1,0:T(8,128)(2,1)S(1)}, u32[]{:S(2)}, u32[]{:S(2)}) async-start(bf16[64,8,256]{2,1,0:T(8,128)(2,1)} %bitcast.4), calls=%async_computation | async-start | bytes 524288 | tf_op jit(solution)/shard_map/all_to_all | solution.py:304
  30.0 0.0 collective-permute-done.near
  30.0 0.0 copy-start.1
  30.1 2.4 %collective-permute-start.1 = (bf16[64,3584]{1,0:T(8,128)(2,1)S(1)}, bf16[64,3584]{1,0:T(8,128)(2,1)S(1)}, u32[]{:S(2)}, u32[]{:S(2)}) collective-permute-start(bf16[64,3584]{1,0:T(8,128)(2,1)S(1)} %constant_dynamic-slice_fusion), channel_id=1, source_target_pairs={{0,2},{1,7},{2,4},{3,1},{4,6},{5,3},{6,0},{7,5},{8,10},{9,15},{10,... | collective-permute-start | bytes 1376264 | tf_op jit(solution)/shard_map/ppermute | solution.py:303
  32.4 2.5 %collective-permute-start.2 = (bf16[128,3584]{1,0:T(8,128)(2,1)S(1)}, bf16[128,3584]{1,0:T(8,128)(2,1)S(1)}, u32[]{:S(2)}, u32[]{:S(2)}) collective-permute-start(bf16[128,3584]{1,0:T(8,128)(2,1)S(1)} %collective-permute-done.near), channel_id=1, source_target_pairs={{0,1},{1,0},{2,3},{3,2},{4,5},{5,4},{6,7},{7,6},{8,9},{9,8},{10,11... | collective-permute-start | bytes 2752520 | tf_op jit(solution)/shard_map/ppermute | solution.py:307
  35.0 4.6 %collective-permute-done.1.far = bf16[64,3584]{1,0:T(8,128)(2,1)S(1)} collective-permute-done((bf16[64,3584]{1,0:T(8,128)(2,1)S(1)}, bf16[64,3584]{1,0:T(8,128)(2,1)S(1)}, u32[]{:S(2)}, u32[]{:S(2)}) %collective-permute-start.1) | collective-permute-done | bytes 458784 | tf_op jit(solution)/shard_map/ppermute | solution.py:303
  39.6 0.0 copy-start.3
  39.6 3.5 %collective-permute-start.3 = (bf16[64,3584]{1,0:T(8,128)(2,1)S(1)}, bf16[64,3584]{1,0:T(8,128)(2,1)}, u32[]{:S(2)}, u32[]{:S(2)}) collective-permute-start(bf16[64,3584]{1,0:T(8,128)(2,1)S(1)} %collective-permute-done.1.far), channel_id=1, source_target_pairs={{0,1},{1,0},{2,3},{3,2},{4,5},{5,4},{6,7},{7,6},{8,9},{9,8},{10,11... | collective-permute-start | bytes 1376264 | tf_op jit(solution)/shard_map/ppermute | solution.py:308
  43.7 7.2 %all-to-all-done = bf16[64,8,256]{2,1,0:T(8,128)(2,1)S(1)} async-done(((bf16[64,8,256]{2,1,0:T(8,128)(2,1)}), bf16[64,8,256]{2,1,0:T(8,128)(2,1)S(1)}, u32[]{:S(2)}, u32[]{:S(2)}) %all-to-all-start) | async-done | bytes 262176 | tf_op jit(solution)/shard_map/all_to_all | solution.py:304
  50.9 2.3 %all_gather.9.halo = bf16[1024,256]{1,0:T(8,128)(2,1)} all-gather(bf16[512,256]{1,0:T(8,128)(2,1)S(1)} %bitcast.9), channel_id=1, replica_groups=mesh['x'=4,'z'=16,'y'=4,'core'=2] {'core'}, dimensions={0}, use_global_device_ids=true | all-gather | bytes 786432 | tf_op jit(solution)/shard_map/all_gather | solution.py:309
  53.2 0.0 copy-done
  53.2 0.0 collective-permute-done.3.far_other
  53.2 0.0 collective-permute-done.2.near_other
  53.2 0.0 copy-start.2
  53.2 0.0 copy-done.1
  53.2 0.0 copy-done.3
  53.3 0.9 copy-done.2
  54.2 16.3 %step.1 = (bf16[256,512]{1,0:T(8,128)(2,1)}, bf16[64,32,128]{2,1,0:T(8,128)(2,1)}, f32[256,256]{1,0:T(8,128)}) custom-call(s32[6]{0:T(128)} %tiles.1, s32[1]{0:T(128)S(6)} %copy.16.live, bf16[256,512]{1,0:T(8,128)(2,1)} %nodes.3, bf16[768,512]{1,0:T(8,128)(2,1)} %edges.1, bf16[256,512]{1,0:T(8,128)(2,1)} %cotangent.1, bf16[1024,256]{1,0:T(8,128)(2,1)} %all_gather.9.halo, ...), custom_call_target="tpu_custom_call" | custom-call | tf_op jit(solution)/shard_map/step/pallas_call | solution.py:311
  70.4 37.9 %all_to_all.10.incoming = bf16[64,32,128]{2,1,0:T(8,128)(2,1)} all-to-all(bf16[64,32,128]{2,1,0:T(8,128)(2,1)} %get-tuple-element.13), channel_id=1, replica_groups=mesh['x'=4,'z'=16,'y'=4,'core'=2] {'x','z'}, dimensions={0} | all-to-all | bytes 1048576 | tf_op jit(solution)/shard_map/all_to_all | solution.py:348
  108.3 2.4 %finish.1 = (bf16[256,256]{1,0:T(8,128)(2,1)}, f32[24,64]{1,0:T(8,128)}) custom-call(bf16[64,32,128]{2,1,0:T(8,128)(2,1)} %all_to_all.10.incoming, f32[256,256]{1,0:T(8,128)} %get-tuple-element.14.base, s32[8,64]{1,0:T(8,128)} %bitcast.13), custom_call_target="tpu_custom_call" | custom-call | tf_op jit(solution)/shard_map/finish/pallas_call | solution.py:349
  110.7 4.6 %all_gather.11 = bf16[256,512]{1,0:T(8,128)(2,1)S(1)} all-gather(bf16[256,256]{1,0:T(8,128)(2,1)} %get-tuple-element.15), channel_id=1, replica_groups=mesh['x'=4,'z'=16,'y'=4,'core'=2] {'core'}, dimensions={1}, use_global_device_ids=true | all-gather | bytes 393216 | tf_op jit(solution)/shard_map/all_gather | solution.py:360
  115.3 0.7 copy.17
  (1 shorter events, 0.0 us)
Async XLA Ops:
  12.4 40.8 %copy-start = (bf16[128,3584]{1,0:T(8,128)(2,1)}, bf16[128,3584]{1,0:T(8,128)(2,1)S(1)}, u32[]{:S(2)}) copy-start(bf16[128,3584]{1,0:T(8,128)(2,1)S(1)} %all_gather.10.pair) | copy-start | bytes 2752516
  12.4 17.6 %collective-permute-start = (bf16[128,3584]{1,0:T(8,128)(2,1)S(1)}, bf16[128,3584]{1,0:T(8,128)(2,1)S(1)}, u32[]{:S(2)}, u32[]{:S(2)}) collective-permute-start(bf16[128,3584]{1,0:T(8,128)(2,1)S(1)} %all_gather.10.pair), channel_id=1, source_target_pairs={{0,2},{1,7},{2,4},{3,1},{4,6},{5,3},{6,0},{7,5},{8,10},{9,15},{10,... | collective-permute-start | bytes 2752520 | tf_op jit(solution)/shard_map/ppermute | solution.py:300
  14.3 36.6 %all-to-all-start = ((bf16[64,8,256]{2,1,0:T(8,128)(2,1)}), bf16[64,8,256]{2,1,0:T(8,128)(2,1)S(1)}, u32[]{:S(2)}, u32[]{:S(2)}) async-start(bf16[64,8,256]{2,1,0:T(8,128)(2,1)} %bitcast.4), calls=%async_computation | async-start | bytes 524288 | tf_op jit(solution)/shard_map/all_to_all | solution.py:304
  30.0 23.2 %copy-start.1 = (bf16[128,3584]{1,0:T(8,128)(2,1)}, bf16[128,3584]{1,0:T(8,128)(2,1)S(1)}, u32[]{:S(2)}) copy-start(bf16[128,3584]{1,0:T(8,128)(2,1)S(1)} %collective-permute-done.near) | copy-start | bytes 2752516
  30.1 9.5 %collective-permute-start.1 = (bf16[64,3584]{1,0:T(8,128)(2,1)S(1)}, bf16[64,3584]{1,0:T(8,128)(2,1)S(1)}, u32[]{:S(2)}, u32[]{:S(2)}) collective-permute-start(bf16[64,3584]{1,0:T(8,128)(2,1)S(1)} %constant_dynamic-slice_fusion), channel_id=1, source_target_pairs={{0,2},{1,7},{2,4},{3,1},{4,6},{5,3},{6,0},{7,5},{8,10},{9,15},{10,... | collective-permute-start | bytes 1376264 | tf_op jit(solution)/shard_map/ppermute | solution.py:303
  32.4 20.8 %collective-permute-start.2 = (bf16[128,3584]{1,0:T(8,128)(2,1)S(1)}, bf16[128,3584]{1,0:T(8,128)(2,1)S(1)}, u32[]{:S(2)}, u32[]{:S(2)}) collective-permute-start(bf16[128,3584]{1,0:T(8,128)(2,1)S(1)} %collective-permute-done.near), channel_id=1, source_target_pairs={{0,1},{1,0},{2,3},{3,2},{4,5},{5,4},{6,7},{7,6},{8,9},{9,8},{10,11... | collective-permute-start | bytes 2752520 | tf_op jit(solution)/shard_map/ppermute | solution.py:307
  39.6 13.7 %copy-start.3 = (bf16[64,3584]{1,0:T(8,128)(2,1)}, bf16[64,3584]{1,0:T(8,128)(2,1)S(1)}, u32[]{:S(2)}) copy-start(bf16[64,3584]{1,0:T(8,128)(2,1)S(1)} %collective-permute-done.1.far) | copy-start | bytes 1376260
  39.6 13.6 %collective-permute-start.3 = (bf16[64,3584]{1,0:T(8,128)(2,1)S(1)}, bf16[64,3584]{1,0:T(8,128)(2,1)}, u32[]{:S(2)}, u32[]{:S(2)}) collective-permute-start(bf16[64,3584]{1,0:T(8,128)(2,1)S(1)} %collective-permute-done.1.far), channel_id=1, source_target_pairs={{0,1},{1,0},{2,3},{3,2},{4,5},{5,4},{6,7},{7,6},{8,9},{9,8},{10,11... | collective-permute-start | bytes 1376264 | tf_op jit(solution)/shard_map/ppermute | solution.py:308
  53.2 0.9 copy-start.2

commit v3 on v2

--- a/solution.py
+++ b/solution.py
@@ -9,8 +9,11 @@
 epsilon = 1e-05
 bf16 = jnp.bfloat16
 f32 = jnp.float32
-VMEM_LIMIT = 56 * 1024 * 1024
+SUPPLY_VMEM = 60 * 1024 * 1024
+STEP_VMEM = 24 * 1024 * 1024
+FINISH_VMEM = 16 * 1024 * 1024
 CHUNK = 32
+BLOCK = 256
 
 
 def nn(a, b):
@@ -85,17 +88,12 @@
     )
 
 
-def by_rows(total, body):
-    def step(i, carry):
-        body(pl.ds(pl.multiple_of(i * CHUNK, CHUNK), CHUNK))
-        return carry
-
-    lax.fori_loop(0, total // CHUNK, step, 0, unroll=2)
+def by_rows(start, body):
+    for at in range(start, start + BLOCK, CHUNK):
+        body(pl.ds(at, CHUNK))
 
 
 def step_kernel(
-    tiles,
-    live,
     nodes,
     edges,
     cotangent,
@@ -106,7 +104,7 @@
     near_other,
     far_other,
     sender,
-    position,
+    receivers,
     node_out,
     outgoing,
     base,
@@ -145,39 +143,35 @@
     table[:n] = nodes[...]
     table[n:, :half] = halo[:h]
     table[n:, half:] = halo[h:]
-    receiver = jnp.concatenate(
-        [
-            jnp.where(
-                b < live[0], position[b : b + 1, :] + tiles[b] * TILE, -1
-            )
-            for b in range(e // TILE)
-        ],
-        axis=1,
-    )
+    receiver = flat_row(receivers[...])
     received[...] = onehot_rows(receiver, n)
     senders = flat_row(sender[...])
     stacked[:, :d] = edges[...]
     stacked[:, d : 2 * d] = nn(onehot_rows(senders, n + h), table[...]).astype(bf16)
     stacked[:, 2 * d :] = nn(received[...], nodes[...]).astype(bf16)
 
-    wide[...] = to_units(stacked[...], first)
-
     def activate(rows):
         v = wide[rows, :]
         s = sigmoid(v)
         low[rows, :] = (v * s).astype(bf16)
         slope[rows, :] = s * (1.0 + v * (1.0 - s))
 
-    by_rows(e, activate)
-    wide[...] = from_units(low[...], second)
-
     def normalise(rows):
         u, r = normed(wide[rows, :])
         unit[rows, :] = u
         scale[rows, :] = jnp.broadcast_to(r, (CHUNK, TILE))
         low[rows, :] = (edges[rows, :].astype(f32) + u).astype(bf16)
 
-    by_rows(e, normalise)
+    def block(start):
+        return pl.ds(start, BLOCK)
+
+    starts = range(0, e, BLOCK)
+    for at in starts:
+        wide[block(at), :] = to_units(stacked[block(at), :], first)
+        by_rows(at, activate)
+    for at in starts:
+        wide[block(at), :] = from_units(low[block(at), :], second)
+        by_rows(at, normalise)
     back = onehot_columns(receiver, n)
     aggregated = nn(back, low[...]).astype(bf16)
 
@@ -196,18 +190,18 @@
         d_preact_node, pl.ds(pl.multiple_of(3 * d + core * half, half), half)
     )
 
-    wide[...] = nn(received[...], d_aggregated)
-
     def denormalise(rows):
         low[rows, :] = normed_back(wide[rows, :], unit[rows, :], scale[rows, :1]).astype(bf16)
 
-    by_rows(e, denormalise)
-    wide[...] = to_units(low[...], second)
-
     def deactivate(rows):
         low[rows, :] = (wide[rows, :] * slope[rows, :]).astype(bf16)
 
-    by_rows(e, deactivate)
+    for at in starts:
+        wide[block(at), :] = nn(received[block(at), :], d_aggregated)
+        by_rows(at, denormalise)
+    for at in starts:
+        wide[block(at), :] = to_units(low[block(at), :], second)
+        by_rows(at, deactivate)
 
     own = units // 8
     pick = (
@@ -236,6 +230,39 @@
         ],
         axis=1,
     ).astype(bf16)
+
+
+def run_step(
+    nodes, edges, cotangent, halo, pair, near, far, near_other, far_other, sender, receivers
+):
+    n, d = nodes.shape
+    e = edges.shape[0]
+    h = halo.shape[0] // 2
+    units = 4 * pair.shape[0]
+    vmem = pl.BlockSpec(memory_space=pltpu.VMEM)
+    return pl.pallas_call(
+        step_kernel,
+        out_shape=(
+            jax.ShapeDtypeStruct((n, d), bf16),
+            jax.ShapeDtypeStruct((64, 32, TILE), bf16),
+            jax.ShapeDtypeStruct((n, d // 2), f32),
+        ),
+        in_specs=[vmem] * 11,
+        out_specs=(vmem, vmem, vmem),
+        scratch_shapes=[
+            pltpu.VMEM((n + h, d), bf16),
+            pltpu.VMEM((e, 3 * d), bf16),
+            pltpu.VMEM((e, units), f32),
+            pltpu.VMEM((e, units), f32),
+            pltpu.VMEM((e, d), f32),
+            pltpu.VMEM((e, TILE), f32),
+            pltpu.VMEM((e, units), bf16),
+            pltpu.VMEM((e, n), bf16),
+            pltpu.VMEM((units, pair.shape[1]), bf16),
+        ],
+        compiler_params=pltpu.CompilerParams(vmem_limit_bytes=STEP_VMEM),
+        name="step",
+    )(nodes, edges, cotangent, halo, pair, near, far, near_other, far_other, sender, receivers)
 
 
 def finish_kernel(incoming, base, send, node_grad, first_grad):
@@ -273,11 +300,8 @@
     h = peers * slots
     columns = lax.axis_size("y")
     own = edge_second.shape[0]
-    units = own * columns * lax.axis_size("core")
     width = edge_first.shape[0] + node_first.shape[0] + 2 * d
     vmem = pl.BlockSpec(memory_space=pltpu.VMEM)
-    smem = pl.BlockSpec(memory_space=pltpu.SMEM)
-    params = pltpu.CompilerParams(vmem_limit_bytes=VMEM_LIMIT)
     send = send_rows[0].T
 
     supply, shard = pl.pallas_call(
@@ -288,7 +312,7 @@
         ),
         in_specs=[vmem] * 6,
         out_specs=(vmem, vmem),
-        compiler_params=params,
+        compiler_params=pltpu.CompilerParams(vmem_limit_bytes=SUPPLY_VMEM),
         name="supply",
     )(nodes, send, edge_first.T, edge_second, node_first.T, node_second)
     pair = lax.all_gather(shard, "core", axis=0, tiled=True)
@@ -308,31 +332,13 @@
     far_other = lax.ppermute(far, "core", [(0, 1), (1, 0)])
     halo = lax.all_gather(received, "core", axis=0, tiled=True)
 
-    node_out, outgoing, base = pl.pallas_call(
-        step_kernel,
-        out_shape=(
-            jax.ShapeDtypeStruct((n, d), bf16),
-            jax.ShapeDtypeStruct((peers, 32, TILE), bf16),
-            jax.ShapeDtypeStruct((n, half), f32),
-        ),
-        in_specs=[smem, smem] + [vmem] * 11,
-        out_specs=(vmem, vmem, vmem),
-        scratch_shapes=[
-            pltpu.VMEM((n + h, d), bf16),
-            pltpu.VMEM((e, 3 * d), bf16),
-            pltpu.VMEM((e, units), f32),
-            pltpu.VMEM((e, units), f32),
-            pltpu.VMEM((e, d), f32),
-            pltpu.VMEM((e, TILE), f32),
-            pltpu.VMEM((e, units), bf16),
-            pltpu.VMEM((e, n), bf16),
-            pltpu.VMEM((units, width), bf16),
-        ],
-        compiler_params=params,
-        name="step",
-    )(
-        block_tile,
-        live_blocks,
+    blocks = block_tile.shape[0]
+    receivers = jnp.where(
+        jnp.arange(blocks, dtype=jnp.int32)[:, None] < live_blocks,
+        receiver_pos.reshape(blocks, TILE) + block_tile[:, None] * TILE,
+        -1,
+    )
+    node_out, outgoing, base = run_step(
         nodes,
         edges,
         node_cotangent,
@@ -342,8 +348,8 @@
         far,
         near_other,
         far_other,
-        sender.reshape(e // TILE, TILE),
-        receiver_pos.reshape(e // TILE, TILE),
+        sender.reshape(blocks, TILE),
+        receivers,
     )
     incoming = lax.all_to_all(outgoing, ("x", "z"), split_axis=0, concat_axis=0, tiled=True)
     half_grad, first_grad = pl.pallas_call(
@@ -354,7 +360,7 @@
         ),
         in_specs=[vmem] * 3,
         out_specs=(vmem, vmem),
-        compiler_params=params,
+        compiler_params=pltpu.CompilerParams(vmem_limit_bytes=FINISH_VMEM),
         name="finish",
     )(incoming, base, send)
     node_grad = lax.all_gather(half_grad, "core", axis=1, tiled=True)

time: 116 us -> 107 us (0.922)
  Pallas kernels: 21.2 us -> 13.2 us
    pallas_call x1, Pallas kernels: 16.3 us -> 9.43 us  [run_step(): pl.pallas_call(step_kernel, out_shape=(jax.ShapeDtypeStruct((n, d), bf16)...]
    pallas_call x1, Pallas kernels: 2.36 us -> 1.12 us  [per_device(): pl.pallas_call(finish_kernel, out_shape=(jax.ShapeDtypeStruct((n, half),...]
where the time goes in v3:
time: 107 us
  blocking collectives  53.5 us (50%)
  starting transfers between devices  26.3 us (25%)
  Pallas kernels  13.2 us (12%)
  waiting for transfers between devices  11.4 us (11%)
  between operations  1.43 us (1%)
    all_to_all x1, blocking collectives, per_device(): lax.all_to_all(outgoing, ('x', 'z'), split_axis=0, concat_axis=0, tiled=T...  37.5 us
    all_to_all x1, starting transfers between devices, per_device(): lax.all_to_all(supply.reshape(peers, slots, half), ('x', 'z'), split_axis...  15.9 us
    pallas_call x1, Pallas kernels, run_step(): pl.pallas_call(step_kernel, out_shape=(jax.ShapeDtypeStruct((n, d), bf16)...  9.43 us
    all_gather x1, blocking collectives, per_device(): pair = lax.all_gather(shard, 'core', axis=0, tiled=True)  9.17 us
    all_to_all x1, waiting for transfers between devices, per_device(): lax.all_to_all(supply.reshape(peers, slots, half), ('x', 'z'), split_axis...  7.33 us
    all_gather x1, blocking collectives, per_device(): node_grad = lax.all_gather(half_grad, 'core', axis=1, tiled=True)  4.34 us
    ppermute x1, waiting for transfers between devices, per_device(): far = lax.ppermute(relayed, ('y', 'core'), beside)  4.05 us
    ppermute x1, starting transfers between devices, per_device(): far_other = lax.ppermute(far, 'core', [(0, 1), (1, 0)])  3.46 us
  transfers between devices with their start and end apart: 5, of which 2 were waited for; matrix products, arithmetic and copies ran while one was open for 0% of the time, Pallas kernels for 0%

profile of v3, /device:TPU:1, one launch (start us, length us, event | category | flops | bytes accessed | tf_op | source)
XLA Modules:
  0.0 106.7 jit_solution(6017675068690341396)
XLA Ops:
  0.6 2.6 %supply.1 = (bf16[512,256]{1,0:T(8,128)(2,1)}, bf16[64,3584]{1,0:T(8,128)(2,1)}) custom-call(bf16[256,512]{1,0:T(8,128)(2,1)} %nodes.3, s32[8,64]{1,0:T(8,128)} %bitcast.14, bf16[64,1536]{1,0:T(8,128)(2,1)} %bitcast.17, bf16[64,512]{1,0:T(8,128)(2,1)} %second.1, bf16[64,1024]{1,0:T(8,128)(2,1)} %bitcast.18, bf16[64,512]{1,0:T(8,128)(2,1)} %node_second.1), custom_call_target="tpu_custom_call" | custom-call | tf_op jit(solution)/shard_map/supply/pallas_call | solution.py:307
  3.3 9.2 %all_gather.10.pair = bf16[128,3584]{1,0:T(8,128)(2,1)S(1)} all-gather(bf16[64,3584]{1,0:T(8,128)(2,1)} %get-tuple-element.11), channel_id=1, replica_groups=mesh['x'=4,'z'=16,'y'=4,'core'=2] {'core'}, dimensions={0}, use_global_device_ids=true | all-gather | bytes 1376256 | tf_op jit(solution)/shard_map/all_gather | solution.py:318
  12.4 1.9 %collective-permute-start = (bf16[128,3584]{1,0:T(8,128)(2,1)S(1)}, bf16[128,3584]{1,0:T(8,128)(2,1)S(1)}, u32[]{:S(2)}, u32[]{:S(2)}) collective-permute-start(bf16[128,3584]{1,0:T(8,128)(2,1)S(1)} %all_gather.10.pair), channel_id=1, source_target_pairs={{0,2},{1,7},{2,4},{3,1},{4,6},{5,3},{6,0},{7,5},{8,10},{9,15},{10,... | collective-permute-start | bytes 2752520 | tf_op jit(solution)/shard_map/ppermute | solution.py:324
  14.3 15.9 %all-to-all-start = ((bf16[64,8,256]{2,1,0:T(8,128)(2,1)}), bf16[64,8,256]{2,1,0:T(8,128)(2,1)}, u32[]{:S(2)}, u32[]{:S(2)}) async-start(bf16[64,8,256]{2,1,0:T(8,128)(2,1)} %bitcast.4), calls=%async_computation | async-start | bytes 524288 | tf_op jit(solution)/shard_map/all_to_all | solution.py:328
  30.3 0.0 copy-start.1
  30.3 0.0 collective-permute-done.near
  30.3 0.0 copy-start.6
  30.3 0.0 copy-start.5
  30.3 2.5 %collective-permute-start.1 = (bf16[64,3584]{1,0:T(8,128)(2,1)S(1)}, bf16[64,3584]{1,0:T(8,128)(2,1)}, u32[]{:S(2)}, u32[]{:S(2)}) collective-permute-start(bf16[64,3584]{1,0:T(8,128)(2,1)S(1)} %constant_dynamic-slice_fusion), channel_id=1, source_target_pairs={{0,2},{1,7},{2,4},{3,1},{4,6},{5,3},{6,0},{7,5},{8,10},{9,15},{10,... | collective-permute-start | bytes 1376264 | tf_op jit(solution)/shard_map/ppermute | solution.py:327
  32.9 2.5 %collective-permute-start.2 = (bf16[128,3584]{1,0:T(8,128)(2,1)S(1)}, bf16[128,3584]{1,0:T(8,128)(2,1)S(1)}, u32[]{:S(2)}, u32[]{:S(2)}) collective-permute-start(bf16[128,3584]{1,0:T(8,128)(2,1)S(1)} %collective-permute-done.near), channel_id=1, source_target_pairs={{0,1},{1,0},{2,3},{3,2},{4,5},{5,4},{6,7},{7,6},{8,9},{9,8},{10,11... | collective-permute-start | bytes 2752520 | tf_op jit(solution)/shard_map/ppermute | solution.py:331
  36.0 0.0 copy-done.6
  36.1 4.0 %collective-permute-done.1.far = bf16[64,3584]{1,0:T(8,128)(2,1)} collective-permute-done((bf16[64,3584]{1,0:T(8,128)(2,1)S(1)}, bf16[64,3584]{1,0:T(8,128)(2,1)}, u32[]{:S(2)}, u32[]{:S(2)}) %collective-permute-start.1) | collective-permute-done | bytes 458784 | tf_op jit(solution)/shard_map/ppermute | solution.py:327
  40.1 3.5 %collective-permute-start.3 = (bf16[64,3584]{1,0:T(8,128)(2,1)}, bf16[64,3584]{1,0:T(8,128)(2,1)}, u32[]{:S(2)}, u32[]{:S(2)}) collective-permute-start(bf16[64,3584]{1,0:T(8,128)(2,1)} %collective-permute-done.1.far), channel_id=1, source_target_pairs={{0,1},{1,0},{2,3},{3,2},{4,5},{5,4},{6,7},{7,6},{8,9},{9,8},{10,11... | collective-permute-start | bytes 1376264 | tf_op jit(solution)/shard_map/ppermute | solution.py:332
  43.6 0.0 copy-done.5
  43.6 0.1 fusion.receivers
  43.7 7.3 %all-to-all-done = bf16[64,8,256]{2,1,0:T(8,128)(2,1)} async-done(((bf16[64,8,256]{2,1,0:T(8,128)(2,1)}), bf16[64,8,256]{2,1,0:T(8,128)(2,1)}, u32[]{:S(2)}, u32[]{:S(2)}) %all-to-all-start) | async-done | bytes 262176 | tf_op jit(solution)/shard_map/all_to_all | solution.py:328
  51.0 0.0 copy-start
  51.0 0.0 copy-start.2
  51.0 0.0 copy-start.4
  51.0 2.5 %all_gather.9.halo = bf16[1024,256]{1,0:T(8,128)(2,1)S(1)} all-gather(bf16[512,256]{1,0:T(8,128)(2,1)} %bitcast.5), channel_id=1, replica_groups=mesh['x'=4,'z'=16,'y'=4,'core'=2] {'core'}, dimensions={0}, use_global_device_ids=true | all-gather | bytes 786432 | tf_op jit(solution)/shard_map/all_gather | solution.py:333
  53.5 0.0 collective-permute-done.3.far_other
  53.5 0.0 collective-permute-done.2.near_other
  53.5 0.0 copy-done.1
  53.5 0.0 copy-done
  53.6 0.0 copy-done.2
  53.6 0.0 copy-done.4
  53.6 9.4 %step.1 = (bf16[256,512]{1,0:T(8,128)(2,1)}, bf16[64,32,128]{2,1,0:T(8,128)(2,1)S(1)}, f32[256,256]{1,0:T(8,128)S(1)}) custom-call(bf16[256,512]{1,0:T(8,128)(2,1)S(1)} %copy-done, bf16[768,512]{1,0:T(8,128)(2,1)S(1)} %copy-done.1, bf16[256,512]{1,0:T(8,128)(2,1)S(1)} %copy-done.2, bf16[1024,256]{1,0:T(8,128)(2,1)S(1)} %all_gather.9.halo, ...), custom_call_target="tpu_custom_call" | custom-call | tf_op jit(solution)/shard_map/step/pallas_call | solution.py:243
  63.0 0.0 copy-start.3
  63.0 37.5 %all_to_all.10.incoming = bf16[64,32,128]{2,1,0:T(8,128)(2,1)S(1)} all-to-all(bf16[64,32,128]{2,1,0:T(8,128)(2,1)S(1)} %get-tuple-element.13), channel_id=1, replica_groups=mesh['x'=4,'z'=16,'y'=4,'core'=2] {'x','z'}, dimensions={0} | all-to-all | bytes 1048576 | tf_op jit(solution)/shard_map/all_to_all | solution.py:354
  100.5 0.0 copy-done.3
  100.5 1.1 %finish.1 = (bf16[256,256]{1,0:T(8,128)(2,1)S(1)}, f32[24,64]{1,0:T(8,128)}) custom-call(bf16[64,32,128]{2,1,0:T(8,128)(2,1)S(1)} %all_to_all.10.incoming, f32[256,256]{1,0:T(8,128)S(1)} %get-tuple-element.14.base, s32[8,64]{1,0:T(8,128)S(1)} %bitcast.15), custom_call_target="tpu_custom_call" | custom-call | tf_op jit(solution)/shard_map/finish/pallas_call | solution.py:355
  101.6 4.3 %all_gather.11 = bf16[256,512]{1,0:T(8,128)(2,1)S(1)} all-gather(bf16[256,256]{1,0:T(8,128)(2,1)S(1)} %get-tuple-element.15), channel_id=1, replica_groups=mesh['x'=4,'z'=16,'y'=4,'core'=2] {'core'}, dimensions={1}, use_global_device_ids=true | all-gather | bytes 393216 | tf_op jit(solution)/shard_map/all_gather | solution.py:366
  106.0 0.7 copy.17
  (3 shorter events, 0.0 us)
Async XLA Ops:
  12.4 17.8 %collective-permute-start = (bf16[128,3584]{1,0:T(8,128)(2,1)S(1)}, bf16[128,3584]{1,0:T(8,128)(2,1)S(1)}, u32[]{:S(2)}, u32[]{:S(2)}) collective-permute-start(bf16[128,3584]{1,0:T(8,128)(2,1)S(1)} %all_gather.10.pair), channel_id=1, source_target_pairs={{0,2},{1,7},{2,4},{3,1},{4,6},{5,3},{6,0},{7,5},{8,10},{9,15},{10,... | collective-permute-start | bytes 2752520 | tf_op jit(solution)/shard_map/ppermute | solution.py:324
  14.3 36.7 %all-to-all-start = ((bf16[64,8,256]{2,1,0:T(8,128)(2,1)}), bf16[64,8,256]{2,1,0:T(8,128)(2,1)}, u32[]{:S(2)}, u32[]{:S(2)}) async-start(bf16[64,8,256]{2,1,0:T(8,128)(2,1)} %bitcast.4), calls=%async_computation | async-start | bytes 524288 | tf_op jit(solution)/shard_map/all_to_all | solution.py:328
  30.3 23.3 %copy-start.1 = (bf16[768,512]{1,0:T(8,128)(2,1)S(1)}, bf16[768,512]{1,0:T(8,128)(2,1)}, u32[]{:S(2)}) copy-start(bf16[768,512]{1,0:T(8,128)(2,1)} %edges.1) | copy-start | bytes 2359300
  30.3 5.8 %copy-start.6 = (s32[6]{0:T(128)S(1)}, s32[6]{0:T(128)}, u32[]{:S(2)}) copy-start(s32[6]{0:T(128)} %param.21) | copy-start | bytes 76
  30.3 13.2 %copy-start.5 = (s32[768]{0:T(1024)S(1)}, s32[768]{0:T(1024)}, u32[]{:S(2)}) copy-start(s32[768]{0:T(1024)} %param.20) | copy-start | bytes 9220
  30.3 9.8 %collective-permute-start.1 = (bf16[64,3584]{1,0:T(8,128)(2,1)S(1)}, bf16[64,3584]{1,0:T(8,128)(2,1)}, u32[]{:S(2)}, u32[]{:S(2)}) collective-permute-start(bf16[64,3584]{1,0:T(8,128)(2,1)S(1)} %constant_dynamic-slice_fusion), channel_id=1, source_target_pairs={{0,2},{1,7},{2,4},{3,1},{4,6},{5,3},{6,0},{7,5},{8,10},{9,15},{10,... | collective-permute-start | bytes 1376264 | tf_op jit(solution)/shard_map/ppermute | solution.py:327
  32.9 20.7 %collective-permute-start.2 = (bf16[128,3584]{1,0:T(8,128)(2,1)S(1)}, bf16[128,3584]{1,0:T(8,128)(2,1)S(1)}, u32[]{:S(2)}, u32[]{:S(2)}) collective-permute-start(bf16[128,3584]{1,0:T(8,128)(2,1)S(1)} %collective-permute-done.near), channel_id=1, source_target_pairs={{0,1},{1,0},{2,3},{3,2},{4,5},{5,4},{6,7},{7,6},{8,9},{9,8},{10,11... | collective-permute-start | bytes 2752520 | tf_op jit(solution)/shard_map/ppermute | solution.py:331
  40.1 13.4 %collective-permute-start.3 = (bf16[64,3584]{1,0:T(8,128)(2,1)}, bf16[64,3584]{1,0:T(8,128)(2,1)}, u32[]{:S(2)}, u32[]{:S(2)}) collective-permute-start(bf16[64,3584]{1,0:T(8,128)(2,1)} %collective-permute-done.1.far), channel_id=1, source_target_pairs={{0,1},{1,0},{2,3},{3,2},{4,5},{5,4},{6,7},{7,6},{8,9},{9,8},{10,11... | collective-permute-start | bytes 1376264 | tf_op jit(solution)/shard_map/ppermute | solution.py:332
  51.0 2.6 %copy-start = (bf16[256,512]{1,0:T(8,128)(2,1)S(1)}, bf16[256,512]{1,0:T(8,128)(2,1)}, u32[]{:S(2)}) copy-start(bf16[256,512]{1,0:T(8,128)(2,1)} %nodes.3) | copy-start | bytes 786436
  51.0 2.6 %copy-start.2 = (bf16[256,512]{1,0:T(8,128)(2,1)S(1)}, bf16[256,512]{1,0:T(8,128)(2,1)}, u32[]{:S(2)}) copy-start(bf16[256,512]{1,0:T(8,128)(2,1)} %cotangent.1) | copy-start | bytes 786436
  51.0 2.6 %copy-start.4 = (s32[768]{0:T(1024)S(1)}, s32[768]{0:T(1024)}, u32[]{:S(2)}) copy-start(s32[768]{0:T(1024)} %param.19) | copy-start | bytes 9220
  63.0 37.5 %copy-start.3 = (s32[1,64,8]{1,2,0:T(8,128)S(1)}, s32[1,64,8]{1,2,0:T(8,128)}, u32[]{:S(2)}) copy-start(s32[1,64,8]{1,2,0:T(8,128)} %param.23) | copy-start | bytes 6148

commit v4 on v3

--- a/solution.py
+++ b/solution.py
@@ -185,10 +185,12 @@
         to_units(d_node_sum, node_second) * (s * (1.0 + preact_node * (1.0 - s)))
     ).astype(bf16)
     d_aggregated = from_units(d_preact_node, pl.ds(4 * d, d)).astype(bf16)
-    columns = pl.ds(pl.multiple_of(core * half, half), half)
-    base[...] = cotangent[:, columns].astype(f32) + from_units(
-        d_preact_node, pl.ds(pl.multiple_of(3 * d + core * half, half), half)
-    )
+    own = units // 8
+    lane = pl.multiple_of(lax.axis_index("y") * TILE, TILE)
+    direct = cotangent[:, pl.ds(lane, TILE)].astype(f32) + from_units(
+        d_preact_node, pl.ds(3 * d + lane, TILE)
+    )
+    direct = jnp.where(core == 0, direct[:, :own], direct[:, own : 2 * own])
 
     def denormalise(rows):
         low[rows, :] = normed_back(wide[rows, :], unit[rows, :], scale[rows, :1]).astype(bf16)
@@ -203,7 +205,6 @@
         wide[block(at), :] = to_units(low[block(at), :], second)
         by_rows(at, deactivate)
 
-    own = units // 8
     pick = (
         lax.broadcasted_iota(jnp.int32, (units, own), 0)
         == lax.broadcasted_iota(jnp.int32, (units, own), 1) + core * own
@@ -214,22 +215,18 @@
     right = jnp.concatenate([grad[:, 16:], jnp.zeros((64, 8, own), f32)], axis=1)
     packed = jnp.concatenate([left, right], axis=2)
 
-    d_sender = from_units(
-        low[...], pl.ds(pl.multiple_of(d + core * half, half), half)
-    ).astype(bf16)
-    d_receiver = from_units(
-        low[...], pl.ds(pl.multiple_of(2 * d + core * half, half), half)
-    ).astype(bf16)
+    d_sender = from_units(low[...], pl.ds(d + lane, TILE)).astype(bf16)
+    d_receiver = from_units(low[...], pl.ds(2 * d + lane, TILE)).astype(bf16)
     table_grad = nn(onehot_columns(senders, n + h), d_sender)
-    base[...] += table_grad[:n] + nn(back, d_receiver)
-    outgoing[...] = jnp.concatenate(
-        [
-            table_grad[n:, :TILE].reshape(64, 8, TILE),
-            table_grad[n:, TILE:].reshape(64, 8, TILE),
-            packed,
-        ],
-        axis=1,
-    ).astype(bf16)
+    table_grad = jnp.where(core == 0, table_grad[:, :own], table_grad[:, own : 2 * own])
+    receiver_grad = nn(back, d_receiver)
+    base[...] = direct + table_grad[:n] + jnp.where(
+        core == 0, receiver_grad[:, :own], receiver_grad[:, own : 2 * own]
+    )
+    d_own = jnp.where(core == 0, low[:, :own], low[:, own : 2 * own])
+    grad = tn(d_own, stacked[...]).T.reshape(64, 3 * d // 64, own)
+    both = jnp.concatenate([table_grad[n:].reshape(64, 8, own), grad], axis=1)
+    outgoing[...] = jnp.concatenate([both[:, :16], both[:, 16:]], axis=2).astype(bf16)
 
 
 def run_step(
@@ -244,8 +241,8 @@
         step_kernel,
         out_shape=(
             jax.ShapeDtypeStruct((n, d), bf16),
-            jax.ShapeDtypeStruct((64, 32, TILE), bf16),
-            jax.ShapeDtypeStruct((n, d // 2), f32),
+            jax.ShapeDtypeStruct((64, 16, TILE), bf16),
+            jax.ShapeDtypeStruct((n, d // 8), f32),
         ),
         in_specs=[vmem] * 11,
         out_specs=(vmem, vmem, vmem),
@@ -267,16 +264,25 @@
 
 def finish_kernel(incoming, base, send, node_grad, first_grad):
     values = incoming[...].astype(f32)
-    rows = values.shape[0] * 8
-    returned = jnp.concatenate(
-        [values[:, :8].reshape(rows, TILE), values[:, 8:16].reshape(rows, TILE)], axis=1
-    ).astype(bf16)
+    own = first_grad.shape[1]
+    returned = values[:, :8, :own].reshape(values.shape[0] * 8, own).astype(bf16)
     hot = onehot_columns(flat_row(send[...]), base.shape[0])
     by_slot = tn(slot_order(*send.shape), returned).astype(bf16)
-    node_grad[...] = (base[...] + nn(hot, by_slot)).astype(bf16)
-    total = jnp.sum(values[:, 16:], axis=0)
-    own = first_grad.shape[1]
-    first_grad[...] = jnp.concatenate([total[:, :own], total[:8, own:]], axis=0)
+    part = (base[...] + nn(hot, by_slot)).astype(bf16)
+    packed = jnp.concatenate([part[:TILE], part[TILE:]], axis=1)
+    for share in range(node_grad.shape[0]):
+        node_grad[share] = packed
+    total = jnp.sum(values, axis=0)
+    first_grad[...] = jnp.concatenate([total[8:, :own], total[:, own:]], axis=0)
+
+
+def place_kernel(parts, node_grad):
+    own = parts.shape[2] // 2
+    for pair in range(parts.shape[0] // 2):
+        low, high = parts[2 * pair], parts[2 * pair + 1]
+        columns = pl.ds(pair * TILE, TILE)
+        node_grad[:TILE, columns] = jnp.concatenate([low[:, :own], high[:, :own]], axis=1)
+        node_grad[TILE:, columns] = jnp.concatenate([low[:, own:], high[:, own:]], axis=1)
 
 
 def per_device(
@@ -352,10 +358,10 @@
         receivers,
     )
     incoming = lax.all_to_all(outgoing, ("x", "z"), split_axis=0, concat_axis=0, tiled=True)
-    half_grad, first_grad = pl.pallas_call(
+    copies, first_grad = pl.pallas_call(
         finish_kernel,
         out_shape=(
-            jax.ShapeDtypeStruct((n, half), bf16),
+            jax.ShapeDtypeStruct((2 * columns, TILE, TILE), bf16),
             jax.ShapeDtypeStruct((edge_first.shape[0] // peers, own), f32),
         ),
         in_specs=[vmem] * 3,
@@ -363,7 +369,15 @@
         compiler_params=pltpu.CompilerParams(vmem_limit_bytes=FINISH_VMEM),
         name="finish",
     )(incoming, base, send)
-    node_grad = lax.all_gather(half_grad, "core", axis=1, tiled=True)
+    parts = lax.all_to_all(copies, ("y", "core"), split_axis=0, concat_axis=0, tiled=True)
+    node_grad = pl.pallas_call(
+        place_kernel,
+        out_shape=jax.ShapeDtypeStruct((n, d), bf16),
+        in_specs=[vmem],
+        out_specs=vmem,
+        compiler_params=pltpu.CompilerParams(vmem_limit_bytes=FINISH_VMEM),
+        name="place",
+    )(parts)
     return (node_out, node_grad, first_grad)
 
 

time: 107 us -> 103 us (0.963)
  blocking collectives: 53.5 us -> 50.2 us
    all_to_all x0 -> x1, blocking collectives: none -> 11 us  [per_device(): lax.all_to_all(copies, ('y', 'core'), split_axis=0, concat_axis=0, tiled=...]
    all_to_all x1, blocking collectives: 37.5 us -> 27.5 us  [per_device(): lax.all_to_all(outgoing, ('x', 'z'), split_axis=0, concat_axis=0, tiled=T...]
    all_gather x1 -> x0, blocking collectives: 4.34 us -> none  [per_device(): node_grad = lax.all_gather(half_grad, 'core', axis=1, tiled=True)]
where the time goes in v4:
time: 103 us
  blocking collectives  50.2 us (49%)
  starting transfers between devices  26.3 us (26%)
  Pallas kernels  13.1 us (13%)
  waiting for transfers between devices  11.4 us (11%)
  between operations  1.43 us (1%)
    all_to_all x1, blocking collectives, per_device(): lax.all_to_all(outgoing, ('x', 'z'), split_axis=0, concat_axis=0, tiled=T...  27.5 us
    all_to_all x1, starting transfers between devices, per_device(): lax.all_to_all(supply.reshape(peers, slots, half), ('x', 'z'), split_axis...  15.9 us
    all_to_all x1, blocking collectives, per_device(): lax.all_to_all(copies, ('y', 'core'), split_axis=0, concat_axis=0, tiled=...  11 us
    all_gather x1, blocking collectives, per_device(): pair = lax.all_gather(shard, 'core', axis=0, tiled=True)  9.17 us
    pallas_call x1, Pallas kernels, run_step(): pl.pallas_call(step_kernel, out_shape=(jax.ShapeDtypeStruct((n, d), bf16)...  8.37 us
    all_to_all x1, waiting for transfers between devices, per_device(): lax.all_to_all(supply.reshape(peers, slots, half), ('x', 'z'), split_axis...  7.33 us
    ppermute x1, waiting for transfers between devices, per_device(): far = lax.ppermute(relayed, ('y', 'core'), beside)  4.05 us
    ppermute x1, starting transfers between devices, per_device(): far_other = lax.ppermute(far, 'core', [(0, 1), (1, 0)])  3.46 us
  transfers between devices with their start and end apart: 5, of which 2 were waited for; matrix products, arithmetic and copies ran while one was open for 0% of the time, Pallas kernels for 0%

profile of v4, /device:TPU:1, one launch (start us, length us, event | category | flops | bytes accessed | tf_op | source)
XLA Modules:
  0.0 102.6 jit_solution(7094262439516718465)
XLA Ops:
  0.6 2.6 %supply.1 = (bf16[512,256]{1,0:T(8,128)(2,1)}, bf16[64,3584]{1,0:T(8,128)(2,1)}) custom-call(bf16[256,512]{1,0:T(8,128)(2,1)} %nodes.3, s32[8,64]{1,0:T(8,128)} %bitcast.14, bf16[64,1536]{1,0:T(8,128)(2,1)} %bitcast.17, bf16[64,512]{1,0:T(8,128)(2,1)} %second.1, bf16[64,1024]{1,0:T(8,128)(2,1)} %bitcast.18, bf16[64,512]{1,0:T(8,128)(2,1)} %node_second.1), custom_call_target="tpu_custom_call" | custom-call | tf_op jit(solution)/shard_map/supply/pallas_call | solution.py:313
  3.3 9.2 %all_gather.7.pair = bf16[128,3584]{1,0:T(8,128)(2,1)S(1)} all-gather(bf16[64,3584]{1,0:T(8,128)(2,1)} %get-tuple-element.11), channel_id=1, replica_groups=mesh['x'=4,'z'=16,'y'=4,'core'=2] {'core'}, dimensions={0}, use_global_device_ids=true | all-gather | bytes 1376256 | tf_op jit(solution)/shard_map/all_gather | solution.py:324
  12.4 1.9 %collective-permute-start = (bf16[128,3584]{1,0:T(8,128)(2,1)S(1)}, bf16[128,3584]{1,0:T(8,128)(2,1)S(1)}, u32[]{:S(2)}, u32[]{:S(2)}) collective-permute-start(bf16[128,3584]{1,0:T(8,128)(2,1)S(1)} %all_gather.7.pair), channel_id=1, source_target_pairs={{0,2},{1,7},{2,4},{3,1},{4,6},{5,3},{6,0},{7,5},{8,10},{9,15},{10,... | collective-permute-start | bytes 2752520 | tf_op jit(solution)/shard_map/ppermute | solution.py:330
  14.3 15.9 %all-to-all-start = ((bf16[64,8,256]{2,1,0:T(8,128)(2,1)}), bf16[64,8,256]{2,1,0:T(8,128)(2,1)}, u32[]{:S(2)}, u32[]{:S(2)}) async-start(bf16[64,8,256]{2,1,0:T(8,128)(2,1)} %bitcast.4), calls=%async_computation | async-start | bytes 524288 | tf_op jit(solution)/shard_map/all_to_all | solution.py:334
  30.3 0.0 copy-start.1
  30.3 0.0 collective-permute-done.near
  30.3 0.0 copy-start.6
  30.3 0.0 copy-start.5
  30.3 2.5 %collective-permute-start.1 = (bf16[64,3584]{1,0:T(8,128)(2,1)S(1)}, bf16[64,3584]{1,0:T(8,128)(2,1)}, u32[]{:S(2)}, u32[]{:S(2)}) collective-permute-start(bf16[64,3584]{1,0:T(8,128)(2,1)S(1)} %constant_dynamic-slice_fusion), channel_id=1, source_target_pairs={{0,2},{1,7},{2,4},{3,1},{4,6},{5,3},{6,0},{7,5},{8,10},{9,15},{10,... | collective-permute-start | bytes 1376264 | tf_op jit(solution)/shard_map/ppermute | solution.py:333
  32.9 2.5 %collective-permute-start.2 = (bf16[128,3584]{1,0:T(8,128)(2,1)S(1)}, bf16[128,3584]{1,0:T(8,128)(2,1)S(1)}, u32[]{:S(2)}, u32[]{:S(2)}) collective-permute-start(bf16[128,3584]{1,0:T(8,128)(2,1)S(1)} %collective-permute-done.near), channel_id=1, source_target_pairs={{0,1},{1,0},{2,3},{3,2},{4,5},{5,4},{6,7},{7,6},{8,9},{9,8},{10,11... | collective-permute-start | bytes 2752520 | tf_op jit(solution)/shard_map/ppermute | solution.py:337
  36.0 0.0 copy-done.6
  36.1 4.0 %collective-permute-done.1.far = bf16[64,3584]{1,0:T(8,128)(2,1)} collective-permute-done((bf16[64,3584]{1,0:T(8,128)(2,1)S(1)}, bf16[64,3584]{1,0:T(8,128)(2,1)}, u32[]{:S(2)}, u32[]{:S(2)}) %collective-permute-start.1) | collective-permute-done | bytes 458784 | tf_op jit(solution)/shard_map/ppermute | solution.py:333
  40.1 3.5 %collective-permute-start.3 = (bf16[64,3584]{1,0:T(8,128)(2,1)}, bf16[64,3584]{1,0:T(8,128)(2,1)}, u32[]{:S(2)}, u32[]{:S(2)}) collective-permute-start(bf16[64,3584]{1,0:T(8,128)(2,1)} %collective-permute-done.1.far), channel_id=1, source_target_pairs={{0,1},{1,0},{2,3},{3,2},{4,5},{5,4},{6,7},{7,6},{8,9},{9,8},{10,11... | collective-permute-start | bytes 1376264 | tf_op jit(solution)/shard_map/ppermute | solution.py:338
  43.6 0.0 copy-done.5
  43.6 0.1 fusion.receivers
  43.7 7.3 %all-to-all-done = bf16[64,8,256]{2,1,0:T(8,128)(2,1)} async-done(((bf16[64,8,256]{2,1,0:T(8,128)(2,1)}), bf16[64,8,256]{2,1,0:T(8,128)(2,1)}, u32[]{:S(2)}, u32[]{:S(2)}) %all-to-all-start) | async-done | bytes 262176 | tf_op jit(solution)/shard_map/all_to_all | solution.py:334
  51.0 0.0 copy-start
  51.0 0.0 copy-start.2
  51.0 0.0 copy-start.4
  51.0 2.5 %all_gather.6.halo = bf16[1024,256]{1,0:T(8,128)(2,1)S(1)} all-gather(bf16[512,256]{1,0:T(8,128)(2,1)} %bitcast.5), channel_id=1, replica_groups=mesh['x'=4,'z'=16,'y'=4,'core'=2] {'core'}, dimensions={0}, use_global_device_ids=true | all-gather | bytes 786432 | tf_op jit(solution)/shard_map/all_gather | solution.py:339
  53.5 0.0 collective-permute-done.3.far_other
  53.5 0.0 collective-permute-done.2.near_other
  53.5 0.0 copy-done.1
  53.5 0.0 copy-done
  53.6 0.0 copy-done.2
  53.6 0.0 copy-done.4
  53.6 8.4 %step.1 = (bf16[256,512]{1,0:T(8,128)(2,1)}, bf16[64,16,128]{2,1,0:T(8,128)(2,1)S(1)}, f32[256,64]{1,0:T(8,128)S(1)}) custom-call(bf16[256,512]{1,0:T(8,128)(2,1)S(1)} %copy-done, bf16[768,512]{1,0:T(8,128)(2,1)S(1)} %copy-done.1, bf16[256,512]{1,0:T(8,128)(2,1)S(1)} %copy-done.2, bf16[1024,256]{1,0:T(8,128)(2,1)S(1)} %all_gather.6.halo, ...), custom_call_target="tpu_custom_call" | custom-call | tf_op jit(solution)/shard_map/step/pallas_call | solution.py:240
  62.0 0.0 copy-start.3
  62.0 27.5 %all_to_all.15.incoming = bf16[64,16,128]{2,1,0:T(8,128)(2,1)S(1)} all-to-all(bf16[64,16,128]{2,1,0:T(8,128)(2,1)S(1)} %get-tuple-element.13), channel_id=1, replica_groups=mesh['x'=4,'z'=16,'y'=4,'core'=2] {'x','z'}, dimensions={0} | all-to-all | bytes 524288 | tf_op jit(solution)/shard_map/all_to_all | solution.py:360
  89.4 0.0 copy-done.3
  89.5 1.3 %finish.1 = (bf16[8,128,128]{2,1,0:T(8,128)(2,1)S(1)}, f32[24,64]{1,0:T(8,128)}) custom-call(bf16[64,16,128]{2,1,0:T(8,128)(2,1)S(1)} %all_to_all.15.incoming, f32[256,64]{1,0:T(8,128)S(1)} %get-tuple-element.14.base, s32[8,64]{1,0:T(8,128)S(1)} %bitcast.15), custom_call_target="tpu_custom_call" | custom-call | tf_op jit(solution)/shard_map/finish/pallas_call | solution.py:361
  90.7 11.0 %all_to_all.16.parts = bf16[8,128,128]{2,1,0:T(8,128)(2,1)S(1)} all-to-all(bf16[8,128,128]{2,1,0:T(8,128)(2,1)S(1)} %get-tuple-element.15), channel_id=1, replica_groups=mesh['x'=4,'z'=16,'y'=4,'core'=2] {'y','core'}, dimensions={0} | all-to-all | bytes 524288 | tf_op jit(solution)/shard_map/all_to_all | solution.py:372
  101.7 0.8 place.1
  (3 shorter events, 0.0 us)
Async XLA Ops:
  12.4 17.8 %collective-permute-start = (bf16[128,3584]{1,0:T(8,128)(2,1)S(1)}, bf16[128,3584]{1,0:T(8,128)(2,1)S(1)}, u32[]{:S(2)}, u32[]{:S(2)}) collective-permute-start(bf16[128,3584]{1,0:T(8,128)(2,1)S(1)} %all_gather.7.pair), channel_id=1, source_target_pairs={{0,2},{1,7},{2,4},{3,1},{4,6},{5,3},{6,0},{7,5},{8,10},{9,15},{10,... | collective-permute-start | bytes 2752520 | tf_op jit(solution)/shard_map/ppermute | solution.py:330
  14.3 36.7 %all-to-all-start = ((bf16[64,8,256]{2,1,0:T(8,128)(2,1)}), bf16[64,8,256]{2,1,0:T(8,128)(2,1)}, u32[]{:S(2)}, u32[]{:S(2)}) async-start(bf16[64,8,256]{2,1,0:T(8,128)(2,1)} %bitcast.4), calls=%async_computation | async-start | bytes 524288 | tf_op jit(solution)/shard_map/all_to_all | solution.py:334
  30.3 23.3 %copy-start.1 = (bf16[768,512]{1,0:T(8,128)(2,1)S(1)}, bf16[768,512]{1,0:T(8,128)(2,1)}, u32[]{:S(2)}) copy-start(bf16[768,512]{1,0:T(8,128)(2,1)} %edges.1) | copy-start | bytes 2359300
  30.3 5.8 %copy-start.6 = (s32[6]{0:T(128)S(1)}, s32[6]{0:T(128)}, u32[]{:S(2)}) copy-start(s32[6]{0:T(128)} %param.21) | copy-start | bytes 76
  30.3 13.2 %copy-start.5 = (s32[768]{0:T(1024)S(1)}, s32[768]{0:T(1024)}, u32[]{:S(2)}) copy-start(s32[768]{0:T(1024)} %param.20) | copy-start | bytes 9220
  30.3 9.8 %collective-permute-start.1 = (bf16[64,3584]{1,0:T(8,128)(2,1)S(1)}, bf16[64,3584]{1,0:T(8,128)(2,1)}, u32[]{:S(2)}, u32[]{:S(2)}) collective-permute-start(bf16[64,3584]{1,0:T(8,128)(2,1)S(1)} %constant_dynamic-slice_fusion), channel_id=1, source_target_pairs={{0,2},{1,7},{2,4},{3,1},{4,6},{5,3},{6,0},{7,5},{8,10},{9,15},{10,... | collective-permute-start | bytes 1376264 | tf_op jit(solution)/shard_map/ppermute | solution.py:333
  32.9 20.7 %collective-permute-start.2 = (bf16[128,3584]{1,0:T(8,128)(2,1)S(1)}, bf16[128,3584]{1,0:T(8,128)(2,1)S(1)}, u32[]{:S(2)}, u32[]{:S(2)}) collective-permute-start(bf16[128,3584]{1,0:T(8,128)(2,1)S(1)} %collective-permute-done.near), channel_id=1, source_target_pairs={{0,1},{1,0},{2,3},{3,2},{4,5},{5,4},{6,7},{7,6},{8,9},{9,8},{10,11... | collective-permute-start | bytes 2752520 | tf_op jit(solution)/shard_map/ppermute | solution.py:337
  40.1 13.4 %collective-permute-start.3 = (bf16[64,3584]{1,0:T(8,128)(2,1)}, bf16[64,3584]{1,0:T(8,128)(2,1)}, u32[]{:S(2)}, u32[]{:S(2)}) collective-permute-start(bf16[64,3584]{1,0:T(8,128)(2,1)} %collective-permute-done.1.far), channel_id=1, source_target_pairs={{0,1},{1,0},{2,3},{3,2},{4,5},{5,4},{6,7},{7,6},{8,9},{9,8},{10,11... | collective-permute-start | bytes 1376264 | tf_op jit(solution)/shard_map/ppermute | solution.py:338
  51.0 2.6 %copy-start = (bf16[256,512]{1,0:T(8,128)(2,1)S(1)}, bf16[256,512]{1,0:T(8,128)(2,1)}, u32[]{:S(2)}) copy-start(bf16[256,512]{1,0:T(8,128)(2,1)} %nodes.3) | copy-start | bytes 786436
  51.0 2.6 %copy-start.2 = (bf16[256,512]{1,0:T(8,128)(2,1)S(1)}, bf16[256,512]{1,0:T(8,128)(2,1)}, u32[]{:S(2)}) copy-start(bf16[256,512]{1,0:T(8,128)(2,1)} %cotangent.1) | copy-start | bytes 786436
  51.0 2.6 %copy-start.4 = (s32[768]{0:T(1024)S(1)}, s32[768]{0:T(1024)}, u32[]{:S(2)}) copy-start(s32[768]{0:T(1024)} %param.19) | copy-start | bytes 9220
  62.0 27.5 %copy-start.3 = (s32[1,64,8]{1,2,0:T(8,128)S(1)}, s32[1,64,8]{1,2,0:T(8,128)}, u32[]{:S(2)}) copy-start(s32[1,64,8]{1,2,0:T(8,128)} %param.23) | copy-start | bytes 6148

commit v5 on v4

--- a/solution.py
+++ b/solution.py
@@ -100,9 +100,8 @@
     halo,
     pair,
     near,
-    far,
     near_other,
-    far_other,
+    fars,
     sender,
     receivers,
     node_out,
@@ -128,7 +127,7 @@
     node_first = pl.ds(3 * d, 2 * d)
     second = pl.ds(5 * d, d)
     node_second = pl.ds(6 * d, d)
-    parts = (pair, near, far, near_other, far_other)
+    parts = (pair, near, near_other, fars)
     units = 0
     for piece in parts:
         weights[units : units + piece.shape[0], :] = piece[...]
@@ -205,18 +204,11 @@
         wide[block(at), :] = to_units(low[block(at), :], second)
         by_rows(at, deactivate)
 
-    pick = (
-        lax.broadcasted_iota(jnp.int32, (units, own), 0)
-        == lax.broadcasted_iota(jnp.int32, (units, own), 1) + core * own
-    )
-    d_own = nn(low[...], pick.astype(f32).astype(bf16))
-    grad = tn(d_own.astype(bf16), stacked[...]).T.reshape(64, 3 * d // 64, own)
-    left = grad[:, :16]
-    right = jnp.concatenate([grad[:, 16:], jnp.zeros((64, 8, own), f32)], axis=1)
-    packed = jnp.concatenate([left, right], axis=2)
-
-    d_sender = from_units(low[...], pl.ds(d + lane, TILE)).astype(bf16)
-    d_receiver = from_units(low[...], pl.ds(2 * d + lane, TILE)).astype(bf16)
+    tails = jnp.concatenate(
+        [weights[:, pl.ds(d + lane, TILE)], weights[:, pl.ds(2 * d + lane, TILE)]], axis=1
+    )
+    d_tails = nn(low[...], tails).astype(bf16)
+    d_sender, d_receiver = d_tails[:, :TILE], d_tails[:, TILE:]
     table_grad = nn(onehot_columns(senders, n + h), d_sender)
     table_grad = jnp.where(core == 0, table_grad[:, :own], table_grad[:, own : 2 * own])
     receiver_grad = nn(back, d_receiver)
@@ -230,7 +222,7 @@
 
 
 def run_step(
-    nodes, edges, cotangent, halo, pair, near, far, near_other, far_other, sender, receivers
+    nodes, edges, cotangent, halo, pair, near, near_other, fars, sender, receivers
 ):
     n, d = nodes.shape
     e = edges.shape[0]
@@ -244,7 +236,7 @@
             jax.ShapeDtypeStruct((64, 16, TILE), bf16),
             jax.ShapeDtypeStruct((n, d // 8), f32),
         ),
-        in_specs=[vmem] * 11,
+        in_specs=[vmem] * 10,
         out_specs=(vmem, vmem, vmem),
         scratch_shapes=[
             pltpu.VMEM((n + h, d), bf16),
@@ -259,7 +251,7 @@
         ],
         compiler_params=pltpu.CompilerParams(vmem_limit_bytes=STEP_VMEM),
         name="step",
-    )(nodes, edges, cotangent, halo, pair, near, far, near_other, far_other, sender, receivers)
+    )(nodes, edges, cotangent, halo, pair, near, near_other, fars, sender, receivers)
 
 
 def finish_kernel(incoming, base, send, node_grad, first_grad):
@@ -328,14 +320,11 @@
         for c in range(2)
     ]
     near = lax.ppermute(pair, ("y", "core"), beside)
-    start = lax.axis_index("core") * own
-    relayed = lax.dynamic_slice_in_dim(near, start, own, 0)
-    far = lax.ppermute(relayed, ("y", "core"), beside)
+    fars = lax.ppermute(near, ("y", "core"), beside)
     received = lax.all_to_all(
         supply.reshape(peers, slots, half), ("x", "z"), split_axis=0, concat_axis=0, tiled=True
     ).reshape(h, half)
     near_other = lax.ppermute(near, "core", [(0, 1), (1, 0)])
-    far_other = lax.ppermute(far, "core", [(0, 1), (1, 0)])
     halo = lax.all_gather(received, "core", axis=0, tiled=True)
 
     blocks = block_tile.shape[0]
@@ -351,9 +340,8 @@
         halo,
         pair,
         near,
-        far,
         near_other,
-        far_other,
+        fars,
         sender.reshape(blocks, TILE),
         receivers,
     )

time: 103 us -> 102 us (level)
  waiting for transfers between devices: 11.4 us -> 15.1 us
  starting transfers between devices: 26.3 us -> 22.8 us
  blocking collectives: 50.2 us -> 49.1 us
    all_to_all x1, waiting for transfers between devices: 7.33 us -> 15.1 us  [per_device(): lax.all_to_all(supply.reshape(peers, slots, half), ('x', 'z'), split_axis...]
    ppermute x2 -> x1, waiting for transfers between devices: 4.05 us -> 0.01 us  [per_device(): fars = lax.ppermute(near, ('y', 'core'), beside)]
    ppermute x2 -> x1, starting transfers between devices: 5.96 us -> 2.37 us  [per_device(): fars = lax.ppermute(near, ('y', 'core'), beside)]
    all_to_all x1, blocking collectives: 27.5 us -> 25 us  [per_device(): lax.all_to_all(outgoing, ('x', 'z'), split_axis=0, concat_axis=0, tiled=T...]
    all_to_all x1, blocking collectives: 11 us -> 12.2 us  [per_device(): lax.all_to_all(copies, ('y', 'core'), split_axis=0, concat_axis=0, tiled=...]
  transfers between devices with their start and end apart: 5 -> 4, of which waited for: 2 -> 1; matrix products, arithmetic and copies ran while one was open for 0% -> 0% of each run, Pallas kernels for 0% -> 0%
where the time goes in v5:
time: 102 us; the launch traced here: 101 us
  blocking collectives  49.1 us (48%)
  starting transfers between devices  22.8 us (22%)
  waiting for transfers between devices  15.1 us (15%)
  Pallas kernels  12.9 us (13%)
  between operations  1.4 us (1%)
    all_to_all x1, blocking collectives, per_device(): lax.all_to_all(outgoing, ('x', 'z'), split_axis=0, concat_axis=0, tiled=T...  25 us
    all_to_all x1, starting transfers between devices, per_device(): lax.all_to_all(supply.reshape(peers, slots, half), ('x', 'z'), split_axis...  15.9 us
    all_to_all x1, waiting for transfers between devices, per_device(): lax.all_to_all(supply.reshape(peers, slots, half), ('x', 'z'), split_axis...  15.1 us
    all_to_all x1, blocking collectives, per_device(): lax.all_to_all(copies, ('y', 'core'), split_axis=0, concat_axis=0, tiled=...  12.2 us
    all_gather x1, blocking collectives, per_device(): pair = lax.all_gather(shard, 'core', axis=0, tiled=True)  9.31 us
    pallas_call x1, Pallas kernels, run_step(): pl.pallas_call(step_kernel, out_shape=(jax.ShapeDtypeStruct((n, d), bf16)...  8.2 us
    pallas_call x1, Pallas kernels, per_device(): pl.pallas_call(supply_kernel, out_shape=(jax.ShapeDtypeStruct((h, half),...  2.62 us
    all_gather x1, blocking collectives, per_device(): halo = lax.all_gather(received, 'core', axis=0, tiled=True)  2.53 us
  transfers between devices with their start and end apart: 4, of which 1 were waited for; matrix products, arithmetic and copies ran while one was open for 0% of the time, Pallas kernels for 0%

profile of v5, /device:TPU:1, one launch (start us, length us, event | category | flops | bytes accessed | tf_op | source)
XLA Modules:
  0.0 101.4 jit_solution(8700031655528760135)
XLA Ops:
  0.6 2.6 %supply.1 = (bf16[512,256]{1,0:T(8,128)(2,1)}, bf16[64,3584]{1,0:T(8,128)(2,1)}) custom-call(bf16[256,512]{1,0:T(8,128)(2,1)} %nodes.3, s32[8,64]{1,0:T(8,128)} %bitcast.14, bf16[64,1536]{1,0:T(8,128)(2,1)} %bitcast.17, bf16[64,512]{1,0:T(8,128)(2,1)} %second.1, bf16[64,1024]{1,0:T(8,128)(2,1)} %bitcast.18, bf16[64,512]{1,0:T(8,128)(2,1)} %node_second.1), custom_call_target="tpu_custom_call" | custom-call | tf_op jit(solution)/shard_map/supply/pallas_call | solution.py:305
  3.3 0.0 copy-start.6
  3.3 0.0 copy-start.5
  3.3 9.3 %all_gather.7.pair = bf16[128,3584]{1,0:T(8,128)(2,1)S(1)} all-gather(bf16[64,3584]{1,0:T(8,128)(2,1)} %get-tuple-element.11), channel_id=1, replica_groups=mesh['x'=4,'z'=16,'y'=4,'core'=2] {'core'}, dimensions={0}, use_global_device_ids=true | all-gather | bytes 1376256 | tf_op jit(solution)/shard_map/all_gather | solution.py:316
  12.6 0.0 copy-start.1
  12.6 2.0 %collective-permute-start = (bf16[128,3584]{1,0:T(8,128)(2,1)S(1)}, bf16[128,3584]{1,0:T(8,128)(2,1)S(1)}, u32[]{:S(2)}, u32[]{:S(2)}) collective-permute-start(bf16[128,3584]{1,0:T(8,128)(2,1)S(1)} %all_gather.7.pair), channel_id=1, source_target_pairs={{0,2},{1,7},{2,4},{3,1},{4,6},{5,3},{6,0},{7,5},{8,10},{9,15},{10,... | collective-permute-start | bytes 2752520 | tf_op jit(solution)/shard_map/ppermute | solution.py:322
  14.6 15.9 %all-to-all-start = ((bf16[64,8,256]{2,1,0:T(8,128)(2,1)}), bf16[64,8,256]{2,1,0:T(8,128)(2,1)}, u32[]{:S(2)}, u32[]{:S(2)}) async-start(bf16[64,8,256]{2,1,0:T(8,128)(2,1)} %bitcast.4), calls=%async_computation | async-start | bytes 524288 | tf_op jit(solution)/shard_map/all_to_all | solution.py:324
  30.5 0.0 collective-permute-done.near
  30.5 2.4 %collective-permute-start.2 = (bf16[128,3584]{1,0:T(8,128)(2,1)S(1)}, bf16[128,3584]{1,0:T(8,128)(2,1)S(1)}, u32[]{:S(2)}, u32[]{:S(2)}) collective-permute-start(bf16[128,3584]{1,0:T(8,128)(2,1)S(1)} %collective-permute-done.near), channel_id=1, source_target_pairs={{0,2},{1,7},{2,4},{3,1},{4,6},{5,3},{6,0},{7,5},{8,10},{9,15},{10,... | collective-permute-start | bytes 2752520 | tf_op jit(solution)/shard_map/ppermute | solution.py:323
  32.9 2.5 %collective-permute-start.1 = (bf16[128,3584]{1,0:T(8,128)(2,1)S(1)}, bf16[128,3584]{1,0:T(8,128)(2,1)}, u32[]{:S(2)}, u32[]{:S(2)}) collective-permute-start(bf16[128,3584]{1,0:T(8,128)(2,1)S(1)} %collective-permute-done.near), channel_id=1, source_target_pairs={{0,1},{1,0},{2,3},{3,2},{4,5},{5,4},{6,7},{7,6},{8,9},{9,8},{10,11... | collective-permute-start | bytes 2752520 | tf_op jit(solution)/shard_map/ppermute | solution.py:327
  36.1 0.0 copy-done.6
  36.1 0.0 copy-done.5
  36.1 0.1 fusion.receivers
  36.2 15.1 %all-to-all-done = bf16[64,8,256]{2,1,0:T(8,128)(2,1)} async-done(((bf16[64,8,256]{2,1,0:T(8,128)(2,1)}), bf16[64,8,256]{2,1,0:T(8,128)(2,1)}, u32[]{:S(2)}, u32[]{:S(2)}) %all-to-all-start) | async-done | bytes 262176 | tf_op jit(solution)/shard_map/all_to_all | solution.py:324
  51.3 0.0 copy-start
  51.3 0.0 copy-start.2
  51.3 0.0 copy-start.4
  51.3 2.5 %all_gather.6.halo = bf16[1024,256]{1,0:T(8,128)(2,1)S(1)} all-gather(bf16[512,256]{1,0:T(8,128)(2,1)} %bitcast.5), channel_id=1, replica_groups=mesh['x'=4,'z'=16,'y'=4,'core'=2] {'core'}, dimensions={0}, use_global_device_ids=true | all-gather | bytes 786432 | tf_op jit(solution)/shard_map/all_gather | solution.py:328
  53.8 0.0 collective-permute-done.2.fars
  53.8 0.0 collective-permute-done.1.near_other
  53.8 0.0 copy-done.1
  53.8 0.0 copy-done
  53.8 0.0 copy-done.2
  53.8 0.0 copy-done.4
  53.9 8.2 %step.1 = (bf16[256,512]{1,0:T(8,128)(2,1)}, bf16[64,16,128]{2,1,0:T(8,128)(2,1)S(1)}, f32[256,64]{1,0:T(8,128)S(1)}) custom-call(bf16[256,512]{1,0:T(8,128)(2,1)S(1)} %copy-done, bf16[768,512]{1,0:T(8,128)(2,1)S(1)} %copy-done.1, bf16[256,512]{1,0:T(8,128)(2,1)S(1)} %copy-done.2, bf16[1024,256]{1,0:T(8,128)(2,1)S(1)} %all_gather.6.halo, ...), custom_call_target="tpu_custom_call" | custom-call | tf_op jit(solution)/shard_map/step/pallas_call | solution.py:232
  62.1 0.0 copy-start.3
  62.1 25.0 %all_to_all.15.incoming = bf16[64,16,128]{2,1,0:T(8,128)(2,1)S(1)} all-to-all(bf16[64,16,128]{2,1,0:T(8,128)(2,1)S(1)} %get-tuple-element.13), channel_id=1, replica_groups=mesh['x'=4,'z'=16,'y'=4,'core'=2] {'x','z'}, dimensions={0} | all-to-all | bytes 524288 | tf_op jit(solution)/shard_map/all_to_all | solution.py:348
  87.1 0.0 copy-done.3
  87.1 1.3 %finish.1 = (bf16[8,128,128]{2,1,0:T(8,128)(2,1)S(1)}, f32[24,64]{1,0:T(8,128)}) custom-call(bf16[64,16,128]{2,1,0:T(8,128)(2,1)S(1)} %all_to_all.15.incoming, f32[256,64]{1,0:T(8,128)S(1)} %get-tuple-element.14.base, s32[8,64]{1,0:T(8,128)S(1)} %bitcast.15), custom_call_target="tpu_custom_call" | custom-call | tf_op jit(solution)/shard_map/finish/pallas_call | solution.py:349
  88.4 12.2 %all_to_all.16.parts = bf16[8,128,128]{2,1,0:T(8,128)(2,1)S(1)} all-to-all(bf16[8,128,128]{2,1,0:T(8,128)(2,1)S(1)} %get-tuple-element.15), channel_id=1, replica_groups=mesh['x'=4,'z'=16,'y'=4,'core'=2] {'y','core'}, dimensions={0} | all-to-all | bytes 524288 | tf_op jit(solution)/shard_map/all_to_all | solution.py:360
  100.6 0.8 place.1
  (2 shorter events, 0.0 us)
Async XLA Ops:
  3.3 32.9 %copy-start.6 = (s32[6]{0:T(128)S(1)}, s32[6]{0:T(128)}, u32[]{:S(2)}) copy-start(s32[6]{0:T(128)} %param.21) | copy-start | bytes 76
  3.3 32.9 %copy-start.5 = (s32[768]{0:T(1024)S(1)}, s32[768]{0:T(1024)}, u32[]{:S(2)}) copy-start(s32[768]{0:T(1024)} %param.20) | copy-start | bytes 9220
  12.6 41.3 %copy-start.1 = (bf16[768,512]{1,0:T(8,128)(2,1)S(1)}, bf16[768,512]{1,0:T(8,128)(2,1)}, u32[]{:S(2)}) copy-start(bf16[768,512]{1,0:T(8,128)(2,1)} %edges.1) | copy-start | bytes 2359300
  12.6 18.0 %collective-permute-start = (bf16[128,3584]{1,0:T(8,128)(2,1)S(1)}, bf16[128,3584]{1,0:T(8,128)(2,1)S(1)}, u32[]{:S(2)}, u32[]{:S(2)}) collective-permute-start(bf16[128,3584]{1,0:T(8,128)(2,1)S(1)} %all_gather.7.pair), channel_id=1, source_target_pairs={{0,2},{1,7},{2,4},{3,1},{4,6},{5,3},{6,0},{7,5},{8,10},{9,15},{10,... | collective-permute-start | bytes 2752520 | tf_op jit(solution)/shard_map/ppermute | solution.py:322
  14.6 36.7 %all-to-all-start = ((bf16[64,8,256]{2,1,0:T(8,128)(2,1)}), bf16[64,8,256]{2,1,0:T(8,128)(2,1)}, u32[]{:S(2)}, u32[]{:S(2)}) async-start(bf16[64,8,256]{2,1,0:T(8,128)(2,1)} %bitcast.4), calls=%async_computation | async-start | bytes 524288 | tf_op jit(solution)/shard_map/all_to_all | solution.py:324
  30.5 23.3 %collective-permute-start.2 = (bf16[128,3584]{1,0:T(8,128)(2,1)S(1)}, bf16[128,3584]{1,0:T(8,128)(2,1)S(1)}, u32[]{:S(2)}, u32[]{:S(2)}) collective-permute-start(bf16[128,3584]{1,0:T(8,128)(2,1)S(1)} %collective-permute-done.near), channel_id=1, source_target_pairs={{0,2},{1,7},{2,4},{3,1},{4,6},{5,3},{6,0},{7,5},{8,10},{9,15},{10,... | collective-permute-start | bytes 2752520 | tf_op jit(solution)/shard_map/ppermute | solution.py:323
  32.9 20.9 %collective-permute-start.1 = (bf16[128,3584]{1,0:T(8,128)(2,1)S(1)}, bf16[128,3584]{1,0:T(8,128)(2,1)}, u32[]{:S(2)}, u32[]{:S(2)}) collective-permute-start(bf16[128,3584]{1,0:T(8,128)(2,1)S(1)} %collective-permute-done.near), channel_id=1, source_target_pairs={{0,1},{1,0},{2,3},{3,2},{4,5},{5,4},{6,7},{7,6},{8,9},{9,8},{10,11... | collective-permute-start | bytes 2752520 | tf_op jit(solution)/shard_map/ppermute | solution.py:327
  51.3 2.6 %copy-start = (bf16[256,512]{1,0:T(8,128)(2,1)S(1)}, bf16[256,512]{1,0:T(8,128)(2,1)}, u32[]{:S(2)}) copy-start(bf16[256,512]{1,0:T(8,128)(2,1)} %nodes.3) | copy-start | bytes 786436
  51.3 2.6 %copy-start.2 = (bf16[256,512]{1,0:T(8,128)(2,1)S(1)}, bf16[256,512]{1,0:T(8,128)(2,1)}, u32[]{:S(2)}) copy-start(bf16[256,512]{1,0:T(8,128)(2,1)} %cotangent.1) | copy-start | bytes 786436
  51.3 2.6 %copy-start.4 = (s32[768]{0:T(1024)S(1)}, s32[768]{0:T(1024)}, u32[]{:S(2)}) copy-start(s32[768]{0:T(1024)} %param.19) | copy-start | bytes 9220
  62.1 25.0 %copy-start.3 = (s32[1,64,8]{1,2,0:T(8,128)S(1)}, s32[1,64,8]{1,2,0:T(8,128)}, u32[]{:S(2)}) copy-start(s32[1,64,8]{1,2,0:T(8,128)} %param.23) | copy-start | bytes 6148

commit v6 on v5

--- a/solution.py
+++ b/solution.py
@@ -116,6 +116,8 @@
     low,
     received,
     weights,
+    fresh,
+    sems,
 ):
     d = nodes.shape[1]
     half = d // 2
@@ -127,11 +129,19 @@
     node_first = pl.ds(3 * d, 2 * d)
     second = pl.ds(5 * d, d)
     node_second = pl.ds(6 * d, d)
-    parts = (pair, near, near_other, fars)
-    units = 0
-    for piece in parts:
-        weights[units : units + piece.shape[0], :] = piece[...]
-        units += piece.shape[0]
+    units = 4 * pair.shape[0]
+    late = [
+        pltpu.make_async_copy(
+            near_other.at[:, columns],
+            weights.at[pl.ds(units - pair.shape[0], pair.shape[0]), columns],
+            sems.at[i],
+        )
+        for i, columns in enumerate((first, pl.ds(3 * d, 4 * d)))
+    ]
+    for copy in late:
+        copy.start()
+    for i, piece in enumerate((pair, near, fars)):
+        weights[i * piece.shape[0] : (i + 1) * piece.shape[0], :] = piece[...]
 
     def to_units(x, columns):
         return nt(x, weights[:, columns])
@@ -165,9 +175,11 @@
         return pl.ds(start, BLOCK)
 
     starts = range(0, e, BLOCK)
+    late[0].wait()
     for at in starts:
         wide[block(at), :] = to_units(stacked[block(at), :], first)
         by_rows(at, activate)
+    late[1].wait()
     for at in starts:
         wide[block(at), :] = from_units(low[block(at), :], second)
         by_rows(at, normalise)
@@ -178,7 +190,9 @@
     s = sigmoid(preact_node)
     hidden_node = (preact_node * s).astype(bf16)
     node_unit, node_scale = normed(from_units(hidden_node, node_second))
-    node_out[...] = (nodes[...].astype(f32) + node_unit).astype(bf16)
+    fresh[...] = (nodes[...].astype(f32) + node_unit).astype(bf16)
+    out_copy = pltpu.make_async_copy(fresh, node_out, sems.at[2])
+    out_copy.start()
     d_node_sum = normed_back(cotangent[...].astype(f32), node_unit, node_scale).astype(bf16)
     d_preact_node = (
         to_units(d_node_sum, node_second) * (s * (1.0 + preact_node * (1.0 - s)))
@@ -219,6 +233,7 @@
     grad = tn(d_own, stacked[...]).T.reshape(64, 3 * d // 64, own)
     both = jnp.concatenate([table_grad[n:].reshape(64, 8, own), grad], axis=1)
     outgoing[...] = jnp.concatenate([both[:, :16], both[:, 16:]], axis=2).astype(bf16)
+    out_copy.wait()
 
 
 def run_step(
@@ -229,6 +244,7 @@
     h = halo.shape[0] // 2
     units = 4 * pair.shape[0]
     vmem = pl.BlockSpec(memory_space=pltpu.VMEM)
+    anywhere = pl.BlockSpec(memory_space=pl.ANY)
     return pl.pallas_call(
         step_kernel,
         out_shape=(
@@ -236,8 +252,8 @@
             jax.ShapeDtypeStruct((64, 16, TILE), bf16),
             jax.ShapeDtypeStruct((n, d // 8), f32),
         ),
-        in_specs=[vmem] * 10,
-        out_specs=(vmem, vmem, vmem),
+        in_specs=[vmem] * 6 + [anywhere] + [vmem] * 3,
+        out_specs=(anywhere, vmem, vmem),
         scratch_shapes=[
             pltpu.VMEM((n + h, d), bf16),
             pltpu.VMEM((e, 3 * d), bf16),
@@ -248,6 +264,8 @@
             pltpu.VMEM((e, units), bf16),
             pltpu.VMEM((e, n), bf16),
             pltpu.VMEM((units, pair.shape[1]), bf16),
+            pltpu.VMEM((n, d), bf16),
+            pltpu.SemaphoreType.DMA((3,)),
         ],
         compiler_params=pltpu.CompilerParams(vmem_limit_bytes=STEP_VMEM),
         name="step",

time: 102 us -> 102 us (level)
  no operation moved by 1% of the time
where the time goes in v6:
time: 102 us; the launch traced here: 101 us
  blocking collectives  49.1 us (48%)
  starting transfers between devices  22.8 us (22%)
  waiting for transfers between devices  15.1 us (15%)
  Pallas kernels  12.6 us (12%)
  between operations  1.4 us (1%)
    all_to_all x1, blocking collectives, per_device(): lax.all_to_all(outgoing, ('x', 'z'), split_axis=0, concat_axis=0, tiled=T...  25 us
    all_to_all x1, starting transfers between devices, per_device(): lax.all_to_all(supply.reshape(peers, slots, half), ('x', 'z'), split_axis...  15.9 us
    all_to_all x1, waiting for transfers between devices, per_device(): lax.all_to_all(supply.reshape(peers, slots, half), ('x', 'z'), split_axis...  15.1 us
    all_to_all x1, blocking collectives, per_device(): lax.all_to_all(copies, ('y', 'core'), split_axis=0, concat_axis=0, tiled=...  12.2 us
    all_gather x1, blocking collectives, per_device(): pair = lax.all_gather(shard, 'core', axis=0, tiled=True)  9.31 us
    pallas_call x1, Pallas kernels, run_step(): pl.pallas_call(step_kernel, out_shape=(jax.ShapeDtypeStruct((n, d), bf16)...  7.87 us
    pallas_call x1, Pallas kernels, per_device(): pl.pallas_call(supply_kernel, out_shape=(jax.ShapeDtypeStruct((h, half),...  2.62 us
    all_gather x1, blocking collectives, per_device(): halo = lax.all_gather(received, 'core', axis=0, tiled=True)  2.53 us
  transfers between devices with their start and end apart: 4, of which 1 were waited for; matrix products, arithmetic and copies ran while one was open for 0% of the time, Pallas kernels for 0%

profile of v6, /device:TPU:1, one launch (start us, length us, event | category | flops | bytes accessed | tf_op | source)
XLA Modules:
  0.0 101.1 jit_solution(3513709458748160617)
XLA Ops:
  0.6 2.6 %supply.1 = (bf16[512,256]{1,0:T(8,128)(2,1)}, bf16[64,3584]{1,0:T(8,128)(2,1)}) custom-call(bf16[256,512]{1,0:T(8,128)(2,1)} %nodes.3, s32[8,64]{1,0:T(8,128)} %bitcast.14, bf16[64,1536]{1,0:T(8,128)(2,1)} %bitcast.17, bf16[64,512]{1,0:T(8,128)(2,1)} %second.1, bf16[64,1024]{1,0:T(8,128)(2,1)} %bitcast.18, bf16[64,512]{1,0:T(8,128)(2,1)} %node_second.1), custom_call_target="tpu_custom_call" | custom-call | tf_op jit(solution)/shard_map/supply/pallas_call | solution.py:323
  3.3 0.0 copy-start.6
  3.3 0.0 copy-start.5
  3.3 9.3 %all_gather.7.pair = bf16[128,3584]{1,0:T(8,128)(2,1)S(1)} all-gather(bf16[64,3584]{1,0:T(8,128)(2,1)} %get-tuple-element.11), channel_id=1, replica_groups=mesh['x'=4,'z'=16,'y'=4,'core'=2] {'core'}, dimensions={0}, use_global_device_ids=true | all-gather | bytes 1376256 | tf_op jit(solution)/shard_map/all_gather | solution.py:334
  12.6 0.0 copy-start.1
  12.6 2.0 %collective-permute-start = (bf16[128,3584]{1,0:T(8,128)(2,1)S(1)}, bf16[128,3584]{1,0:T(8,128)(2,1)S(1)}, u32[]{:S(2)}, u32[]{:S(2)}) collective-permute-start(bf16[128,3584]{1,0:T(8,128)(2,1)S(1)} %all_gather.7.pair), channel_id=1, source_target_pairs={{0,2},{1,7},{2,4},{3,1},{4,6},{5,3},{6,0},{7,5},{8,10},{9,15},{10,... | collective-permute-start | bytes 2752520 | tf_op jit(solution)/shard_map/ppermute | solution.py:340
  14.6 15.9 %all-to-all-start = ((bf16[64,8,256]{2,1,0:T(8,128)(2,1)}), bf16[64,8,256]{2,1,0:T(8,128)(2,1)}, u32[]{:S(2)}, u32[]{:S(2)}) async-start(bf16[64,8,256]{2,1,0:T(8,128)(2,1)} %bitcast.4), calls=%async_computation | async-start | bytes 524288 | tf_op jit(solution)/shard_map/all_to_all | solution.py:342
  30.5 0.0 collective-permute-done.near
  30.5 2.4 %collective-permute-start.2 = (bf16[128,3584]{1,0:T(8,128)(2,1)S(1)}, bf16[128,3584]{1,0:T(8,128)(2,1)S(1)}, u32[]{:S(2)}, u32[]{:S(2)}) collective-permute-start(bf16[128,3584]{1,0:T(8,128)(2,1)S(1)} %collective-permute-done.near), channel_id=1, source_target_pairs={{0,2},{1,7},{2,4},{3,1},{4,6},{5,3},{6,0},{7,5},{8,10},{9,15},{10,... | collective-permute-start | bytes 2752520 | tf_op jit(solution)/shard_map/ppermute | solution.py:341
  32.9 2.5 %collective-permute-start.1 = (bf16[128,3584]{1,0:T(8,128)(2,1)S(1)}, bf16[128,3584]{1,0:T(8,128)(2,1)}, u32[]{:S(2)}, u32[]{:S(2)}) collective-permute-start(bf16[128,3584]{1,0:T(8,128)(2,1)S(1)} %collective-permute-done.near), channel_id=1, source_target_pairs={{0,1},{1,0},{2,3},{3,2},{4,5},{5,4},{6,7},{7,6},{8,9},{9,8},{10,11... | collective-permute-start | bytes 2752520 | tf_op jit(solution)/shard_map/ppermute | solution.py:345
  36.1 0.0 copy-done.6
  36.1 0.0 copy-done.5
  36.1 0.1 fusion.receivers
  36.2 15.1 %all-to-all-done = bf16[64,8,256]{2,1,0:T(8,128)(2,1)} async-done(((bf16[64,8,256]{2,1,0:T(8,128)(2,1)}), bf16[64,8,256]{2,1,0:T(8,128)(2,1)}, u32[]{:S(2)}, u32[]{:S(2)}) %all-to-all-start) | async-done | bytes 262176 | tf_op jit(solution)/shard_map/all_to_all | solution.py:342
  51.3 0.0 copy-start
  51.3 0.0 copy-start.2
  51.3 0.0 copy-start.4
  51.3 2.5 %all_gather.6.halo = bf16[1024,256]{1,0:T(8,128)(2,1)S(1)} all-gather(bf16[512,256]{1,0:T(8,128)(2,1)} %bitcast.5), channel_id=1, replica_groups=mesh['x'=4,'z'=16,'y'=4,'core'=2] {'core'}, dimensions={0}, use_global_device_ids=true | all-gather | bytes 786432 | tf_op jit(solution)/shard_map/all_gather | solution.py:346
  53.8 0.0 collective-permute-done.2.fars
  53.8 0.0 collective-permute-done.1.near_other
  53.8 0.0 copy-done.1
  53.8 0.0 copy-done
  53.8 0.0 copy-done.2
  53.8 0.0 copy-done.4
  53.9 7.9 %step.1 = (bf16[256,512]{1,0:T(8,128)(2,1)}, bf16[64,16,128]{2,1,0:T(8,128)(2,1)S(1)}, f32[256,64]{1,0:T(8,128)S(1)}) custom-call(bf16[256,512]{1,0:T(8,128)(2,1)S(1)} %copy-done, bf16[768,512]{1,0:T(8,128)(2,1)S(1)} %copy-done.1, bf16[256,512]{1,0:T(8,128)(2,1)S(1)} %copy-done.2, bf16[1024,256]{1,0:T(8,128)(2,1)S(1)} %all_gather.6.halo, ...), custom_call_target="tpu_custom_call" | custom-call | tf_op jit(solution)/shard_map/step/pallas_call | solution.py:248
  61.7 0.0 copy-start.3
  61.7 25.0 %all_to_all.15.incoming = bf16[64,16,128]{2,1,0:T(8,128)(2,1)S(1)} all-to-all(bf16[64,16,128]{2,1,0:T(8,128)(2,1)S(1)} %get-tuple-element.13), channel_id=1, replica_groups=mesh['x'=4,'z'=16,'y'=4,'core'=2] {'x','z'}, dimensions={0} | all-to-all | bytes 524288 | tf_op jit(solution)/shard_map/all_to_all | solution.py:366
  86.8 0.0 copy-done.3
  86.8 1.3 %finish.1 = (bf16[8,128,128]{2,1,0:T(8,128)(2,1)S(1)}, f32[24,64]{1,0:T(8,128)}) custom-call(bf16[64,16,128]{2,1,0:T(8,128)(2,1)S(1)} %all_to_all.15.incoming, f32[256,64]{1,0:T(8,128)S(1)} %get-tuple-element.14.base, s32[8,64]{1,0:T(8,128)S(1)} %bitcast.15), custom_call_target="tpu_custom_call" | custom-call | tf_op jit(solution)/shard_map/finish/pallas_call | solution.py:367
  88.0 12.2 %all_to_all.16.parts = bf16[8,128,128]{2,1,0:T(8,128)(2,1)S(1)} all-to-all(bf16[8,128,128]{2,1,0:T(8,128)(2,1)S(1)} %get-tuple-element.15), channel_id=1, replica_groups=mesh['x'=4,'z'=16,'y'=4,'core'=2] {'y','core'}, dimensions={0} | all-to-all | bytes 524288 | tf_op jit(solution)/shard_map/all_to_all | solution.py:378
  100.3 0.8 place.1
  (2 shorter events, 0.0 us)
Async XLA Ops:
  3.3 32.9 %copy-start.6 = (s32[6]{0:T(128)S(1)}, s32[6]{0:T(128)}, u32[]{:S(2)}) copy-start(s32[6]{0:T(128)} %param.21) | copy-start | bytes 76
  3.3 32.9 %copy-start.5 = (s32[768]{0:T(1024)S(1)}, s32[768]{0:T(1024)}, u32[]{:S(2)}) copy-start(s32[768]{0:T(1024)} %param.20) | copy-start | bytes 9220
  12.6 41.3 %copy-start.1 = (bf16[768,512]{1,0:T(8,128)(2,1)S(1)}, bf16[768,512]{1,0:T(8,128)(2,1)}, u32[]{:S(2)}) copy-start(bf16[768,512]{1,0:T(8,128)(2,1)} %edges.1) | copy-start | bytes 2359300
  12.6 18.0 %collective-permute-start = (bf16[128,3584]{1,0:T(8,128)(2,1)S(1)}, bf16[128,3584]{1,0:T(8,128)(2,1)S(1)}, u32[]{:S(2)}, u32[]{:S(2)}) collective-permute-start(bf16[128,3584]{1,0:T(8,128)(2,1)S(1)} %all_gather.7.pair), channel_id=1, source_target_pairs={{0,2},{1,7},{2,4},{3,1},{4,6},{5,3},{6,0},{7,5},{8,10},{9,15},{10,... | collective-permute-start | bytes 2752520 | tf_op jit(solution)/shard_map/ppermute | solution.py:340
  14.6 36.7 %all-to-all-start = ((bf16[64,8,256]{2,1,0:T(8,128)(2,1)}), bf16[64,8,256]{2,1,0:T(8,128)(2,1)}, u32[]{:S(2)}, u32[]{:S(2)}) async-start(bf16[64,8,256]{2,1,0:T(8,128)(2,1)} %bitcast.4), calls=%async_computation | async-start | bytes 524288 | tf_op jit(solution)/shard_map/all_to_all | solution.py:342
  30.5 23.3 %collective-permute-start.2 = (bf16[128,3584]{1,0:T(8,128)(2,1)S(1)}, bf16[128,3584]{1,0:T(8,128)(2,1)S(1)}, u32[]{:S(2)}, u32[]{:S(2)}) collective-permute-start(bf16[128,3584]{1,0:T(8,128)(2,1)S(1)} %collective-permute-done.near), channel_id=1, source_target_pairs={{0,2},{1,7},{2,4},{3,1},{4,6},{5,3},{6,0},{7,5},{8,10},{9,15},{10,... | collective-permute-start | bytes 2752520 | tf_op jit(solution)/shard_map/ppermute | solution.py:341
  32.9 20.9 %collective-permute-start.1 = (bf16[128,3584]{1,0:T(8,128)(2,1)S(1)}, bf16[128,3584]{1,0:T(8,128)(2,1)}, u32[]{:S(2)}, u32[]{:S(2)}) collective-permute-start(bf16[128,3584]{1,0:T(8,128)(2,1)S(1)} %collective-permute-done.near), channel_id=1, source_target_pairs={{0,1},{1,0},{2,3},{3,2},{4,5},{5,4},{6,7},{7,6},{8,9},{9,8},{10,11... | collective-permute-start | bytes 2752520 | tf_op jit(solution)/shard_map/ppermute | solution.py:345
  51.3 2.6 %copy-start = (bf16[256,512]{1,0:T(8,128)(2,1)S(1)}, bf16[256,512]{1,0:T(8,128)(2,1)}, u32[]{:S(2)}) copy-start(bf16[256,512]{1,0:T(8,128)(2,1)} %nodes.3) | copy-start | bytes 786436
  51.3 2.6 %copy-start.2 = (bf16[256,512]{1,0:T(8,128)(2,1)S(1)}, bf16[256,512]{1,0:T(8,128)(2,1)}, u32[]{:S(2)}) copy-start(bf16[256,512]{1,0:T(8,128)(2,1)} %cotangent.1) | copy-start | bytes 786436
  51.3 2.6 %copy-start.4 = (s32[768]{0:T(1024)S(1)}, s32[768]{0:T(1024)}, u32[]{:S(2)}) copy-start(s32[768]{0:T(1024)} %param.19) | copy-start | bytes 9220
  61.7 25.0 %copy-start.3 = (s32[1,64,8]{1,2,0:T(8,128)S(1)}, s32[1,64,8]{1,2,0:T(8,128)}, u32[]{:S(2)}) copy-start(s32[1,64,8]{1,2,0:T(8,128)} %param.23) | copy-start | bytes 6148

commit v7 on v6

--- a/solution.py
+++ b/solution.py
@@ -12,7 +12,7 @@
 SUPPLY_VMEM = 60 * 1024 * 1024
 STEP_VMEM = 24 * 1024 * 1024
 FINISH_VMEM = 16 * 1024 * 1024
-CHUNK = 32
+CHUNK = 16
 BLOCK = 256
 
 
@@ -50,9 +50,14 @@
 
 def slot_order(slots, peers):
     count = slots * peers
-    row = lax.broadcasted_iota(jnp.int32, (count, count), 0)
-    column = lax.broadcasted_iota(jnp.int32, (count, count), 1)
-    return ((row % slots) * peers + row // slots == column).astype(f32).astype(bf16)
+    bits = slots.bit_length() - 1
+    row = lax.broadcasted_iota(jnp.int32, (count, TILE), 0)
+    lanes = lax.broadcasted_iota(jnp.int32, (count, TILE), 1)
+    source = (row & (slots - 1)) * peers + (row >> bits)
+    return jnp.concatenate(
+        [(source == lanes + k * TILE).astype(f32).astype(bf16) for k in range(count // TILE)],
+        axis=1,
+    )
 
 
 def supply_kernel(nodes, send, first, second, node_first, node_second, supply, weights):

time: 102 us -> 101 us (level)
  no operation moved by 1% of the time
where the time goes in v7:
time: 101 us
  blocking collectives  49.1 us (49%)
  starting transfers between devices  22.8 us (23%)
  waiting for transfers between devices  15.1 us (15%)
  Pallas kernels  12.5 us (12%)
  between operations  1.4 us (1%)
    all_to_all x1, blocking collectives, per_device(): lax.all_to_all(outgoing, ('x', 'z'), split_axis=0, concat_axis=0, tiled=T...  25 us
    all_to_all x1, starting transfers between devices, per_device(): lax.all_to_all(supply.reshape(peers, slots, half), ('x', 'z'), split_axis...  15.9 us
    all_to_all x1, waiting for transfers between devices, per_device(): lax.all_to_all(supply.reshape(peers, slots, half), ('x', 'z'), split_axis...  15.1 us
    all_to_all x1, blocking collectives, per_device(): lax.all_to_all(copies, ('y', 'core'), split_axis=0, concat_axis=0, tiled=...  12.2 us
    all_gather x1, blocking collectives, per_device(): pair = lax.all_gather(shard, 'core', axis=0, tiled=True)  9.31 us
    pallas_call x1, Pallas kernels, run_step(): pl.pallas_call(step_kernel, out_shape=(jax.ShapeDtypeStruct((n, d), bf16)...  7.83 us
    pallas_call x1, Pallas kernels, per_device(): pl.pallas_call(supply_kernel, out_shape=(jax.ShapeDtypeStruct((h, half),...  2.62 us
    all_gather x1, blocking collectives, per_device(): halo = lax.all_gather(received, 'core', axis=0, tiled=True)  2.53 us
  transfers between devices with their start and end apart: 4, of which 1 were waited for; matrix products, arithmetic and copies ran while one was open for 0% of the time, Pallas kernels for 0%

profile of v7, /device:TPU:1, one launch (start us, length us, event | category | flops | bytes accessed | tf_op | source)
XLA Modules:
  0.0 101.1 jit_solution(14048806306775362413)
XLA Ops:
  0.6 2.6 %supply.1 = (bf16[512,256]{1,0:T(8,128)(2,1)}, bf16[64,3584]{1,0:T(8,128)(2,1)}) custom-call(bf16[256,512]{1,0:T(8,128)(2,1)} %nodes.3, s32[8,64]{1,0:T(8,128)} %bitcast.14, bf16[64,1536]{1,0:T(8,128)(2,1)} %bitcast.17, bf16[64,512]{1,0:T(8,128)(2,1)} %second.1, bf16[64,1024]{1,0:T(8,128)(2,1)} %bitcast.18, bf16[64,512]{1,0:T(8,128)(2,1)} %node_second.1), custom_call_target="tpu_custom_call" | custom-call | tf_op jit(solution)/shard_map/supply/pallas_call | solution.py:328
  3.3 0.0 copy-start.6
  3.3 0.0 copy-start.5
  3.3 9.3 %all_gather.7.pair = bf16[128,3584]{1,0:T(8,128)(2,1)S(1)} all-gather(bf16[64,3584]{1,0:T(8,128)(2,1)} %get-tuple-element.11), channel_id=1, replica_groups=mesh['x'=4,'z'=16,'y'=4,'core'=2] {'core'}, dimensions={0}, use_global_device_ids=true | all-gather | bytes 1376256 | tf_op jit(solution)/shard_map/all_gather | solution.py:339
  12.6 0.0 copy-start.1
  12.6 2.0 %collective-permute-start = (bf16[128,3584]{1,0:T(8,128)(2,1)S(1)}, bf16[128,3584]{1,0:T(8,128)(2,1)S(1)}, u32[]{:S(2)}, u32[]{:S(2)}) collective-permute-start(bf16[128,3584]{1,0:T(8,128)(2,1)S(1)} %all_gather.7.pair), channel_id=1, source_target_pairs={{0,2},{1,7},{2,4},{3,1},{4,6},{5,3},{6,0},{7,5},{8,10},{9,15},{10,... | collective-permute-start | bytes 2752520 | tf_op jit(solution)/shard_map/ppermute | solution.py:345
  14.6 15.9 %all-to-all-start = ((bf16[64,8,256]{2,1,0:T(8,128)(2,1)}), bf16[64,8,256]{2,1,0:T(8,128)(2,1)}, u32[]{:S(2)}, u32[]{:S(2)}) async-start(bf16[64,8,256]{2,1,0:T(8,128)(2,1)} %bitcast.4), calls=%async_computation | async-start | bytes 524288 | tf_op jit(solution)/shard_map/all_to_all | solution.py:347
  30.5 0.0 collective-permute-done.near
  30.5 2.4 %collective-permute-start.2 = (bf16[128,3584]{1,0:T(8,128)(2,1)S(1)}, bf16[128,3584]{1,0:T(8,128)(2,1)S(1)}, u32[]{:S(2)}, u32[]{:S(2)}) collective-permute-start(bf16[128,3584]{1,0:T(8,128)(2,1)S(1)} %collective-permute-done.near), channel_id=1, source_target_pairs={{0,2},{1,7},{2,4},{3,1},{4,6},{5,3},{6,0},{7,5},{8,10},{9,15},{10,... | collective-permute-start | bytes 2752520 | tf_op jit(solution)/shard_map/ppermute | solution.py:346
  32.9 2.5 %collective-permute-start.1 = (bf16[128,3584]{1,0:T(8,128)(2,1)S(1)}, bf16[128,3584]{1,0:T(8,128)(2,1)}, u32[]{:S(2)}, u32[]{:S(2)}) collective-permute-start(bf16[128,3584]{1,0:T(8,128)(2,1)S(1)} %collective-permute-done.near), channel_id=1, source_target_pairs={{0,1},{1,0},{2,3},{3,2},{4,5},{5,4},{6,7},{7,6},{8,9},{9,8},{10,11... | collective-permute-start | bytes 2752520 | tf_op jit(solution)/shard_map/ppermute | solution.py:350
  36.1 0.0 copy-done.6
  36.1 0.0 copy-done.5
  36.1 0.1 fusion.receivers
  36.2 15.1 %all-to-all-done = bf16[64,8,256]{2,1,0:T(8,128)(2,1)} async-done(((bf16[64,8,256]{2,1,0:T(8,128)(2,1)}), bf16[64,8,256]{2,1,0:T(8,128)(2,1)}, u32[]{:S(2)}, u32[]{:S(2)}) %all-to-all-start) | async-done | bytes 262176 | tf_op jit(solution)/shard_map/all_to_all | solution.py:347
  51.3 0.0 copy-start
  51.3 0.0 copy-start.2
  51.3 0.0 copy-start.4
  51.3 2.5 %all_gather.6.halo = bf16[1024,256]{1,0:T(8,128)(2,1)S(1)} all-gather(bf16[512,256]{1,0:T(8,128)(2,1)} %bitcast.5), channel_id=1, replica_groups=mesh['x'=4,'z'=16,'y'=4,'core'=2] {'core'}, dimensions={0}, use_global_device_ids=true | all-gather | bytes 786432 | tf_op jit(solution)/shard_map/all_gather | solution.py:351
  53.8 0.0 collective-permute-done.2.fars
  53.8 0.0 collective-permute-done.1.near_other
  53.8 0.0 copy-done.1
  53.8 0.0 copy-done
  53.8 0.0 copy-done.2
  53.8 0.0 copy-done.4
  53.9 7.8 %step.1 = (bf16[256,512]{1,0:T(8,128)(2,1)}, bf16[64,16,128]{2,1,0:T(8,128)(2,1)S(1)}, f32[256,64]{1,0:T(8,128)S(1)}) custom-call(bf16[256,512]{1,0:T(8,128)(2,1)S(1)} %copy-done, bf16[768,512]{1,0:T(8,128)(2,1)S(1)} %copy-done.1, bf16[256,512]{1,0:T(8,128)(2,1)S(1)} %copy-done.2, bf16[1024,256]{1,0:T(8,128)(2,1)S(1)} %all_gather.6.halo, ...), custom_call_target="tpu_custom_call" | custom-call | tf_op jit(solution)/shard_map/step/pallas_call | solution.py:253
  61.7 0.0 copy-start.3
  61.7 25.0 %all_to_all.15.incoming = bf16[64,16,128]{2,1,0:T(8,128)(2,1)S(1)} all-to-all(bf16[64,16,128]{2,1,0:T(8,128)(2,1)S(1)} %get-tuple-element.13), channel_id=1, replica_groups=mesh['x'=4,'z'=16,'y'=4,'core'=2] {'x','z'}, dimensions={0} | all-to-all | bytes 524288 | tf_op jit(solution)/shard_map/all_to_all | solution.py:371
  86.7 0.0 copy-done.3
  86.7 1.3 %finish.1 = (bf16[8,128,128]{2,1,0:T(8,128)(2,1)S(1)}, f32[24,64]{1,0:T(8,128)}) custom-call(bf16[64,16,128]{2,1,0:T(8,128)(2,1)S(1)} %all_to_all.15.incoming, f32[256,64]{1,0:T(8,128)S(1)} %get-tuple-element.14.base, s32[8,64]{1,0:T(8,128)S(1)} %bitcast.15), custom_call_target="tpu_custom_call" | custom-call | tf_op jit(solution)/shard_map/finish/pallas_call | solution.py:372
  88.0 12.2 %all_to_all.16.parts = bf16[8,128,128]{2,1,0:T(8,128)(2,1)S(1)} all-to-all(bf16[8,128,128]{2,1,0:T(8,128)(2,1)S(1)} %get-tuple-element.15), channel_id=1, replica_groups=mesh['x'=4,'z'=16,'y'=4,'core'=2] {'y','core'}, dimensions={0} | all-to-all | bytes 524288 | tf_op jit(solution)/shard_map/all_to_all | solution.py:383
  100.2 0.8 place.1
  (2 shorter events, 0.0 us)
Async XLA Ops:
  3.3 32.9 %copy-start.6 = (s32[6]{0:T(128)S(1)}, s32[6]{0:T(128)}, u32[]{:S(2)}) copy-start(s32[6]{0:T(128)} %param.21) | copy-start | bytes 76
  3.3 32.9 %copy-start.5 = (s32[768]{0:T(1024)S(1)}, s32[768]{0:T(1024)}, u32[]{:S(2)}) copy-start(s32[768]{0:T(1024)} %param.20) | copy-start | bytes 9220
  12.6 41.3 %copy-start.1 = (bf16[768,512]{1,0:T(8,128)(2,1)S(1)}, bf16[768,512]{1,0:T(8,128)(2,1)}, u32[]{:S(2)}) copy-start(bf16[768,512]{1,0:T(8,128)(2,1)} %edges.1) | copy-start | bytes 2359300
  12.6 18.0 %collective-permute-start = (bf16[128,3584]{1,0:T(8,128)(2,1)S(1)}, bf16[128,3584]{1,0:T(8,128)(2,1)S(1)}, u32[]{:S(2)}, u32[]{:S(2)}) collective-permute-start(bf16[128,3584]{1,0:T(8,128)(2,1)S(1)} %all_gather.7.pair), channel_id=1, source_target_pairs={{0,2},{1,7},{2,4},{3,1},{4,6},{5,3},{6,0},{7,5},{8,10},{9,15},{10,... | collective-permute-start | bytes 2752520 | tf_op jit(solution)/shard_map/ppermute | solution.py:345
  14.6 36.7 %all-to-all-start = ((bf16[64,8,256]{2,1,0:T(8,128)(2,1)}), bf16[64,8,256]{2,1,0:T(8,128)(2,1)}, u32[]{:S(2)}, u32[]{:S(2)}) async-start(bf16[64,8,256]{2,1,0:T(8,128)(2,1)} %bitcast.4), calls=%async_computation | async-start | bytes 524288 | tf_op jit(solution)/shard_map/all_to_all | solution.py:347
  30.5 23.3 %collective-permute-start.2 = (bf16[128,3584]{1,0:T(8,128)(2,1)S(1)}, bf16[128,3584]{1,0:T(8,128)(2,1)S(1)}, u32[]{:S(2)}, u32[]{:S(2)}) collective-permute-start(bf16[128,3584]{1,0:T(8,128)(2,1)S(1)} %collective-permute-done.near), channel_id=1, source_target_pairs={{0,2},{1,7},{2,4},{3,1},{4,6},{5,3},{6,0},{7,5},{8,10},{9,15},{10,... | collective-permute-start | bytes 2752520 | tf_op jit(solution)/shard_map/ppermute | solution.py:346
  32.9 20.9 %collective-permute-start.1 = (bf16[128,3584]{1,0:T(8,128)(2,1)S(1)}, bf16[128,3584]{1,0:T(8,128)(2,1)}, u32[]{:S(2)}, u32[]{:S(2)}) collective-permute-start(bf16[128,3584]{1,0:T(8,128)(2,1)S(1)} %collective-permute-done.near), channel_id=1, source_target_pairs={{0,1},{1,0},{2,3},{3,2},{4,5},{5,4},{6,7},{7,6},{8,9},{9,8},{10,11... | collective-permute-start | bytes 2752520 | tf_op jit(solution)/shard_map/ppermute | solution.py:350
  51.3 2.6 %copy-start = (bf16[256,512]{1,0:T(8,128)(2,1)S(1)}, bf16[256,512]{1,0:T(8,128)(2,1)}, u32[]{:S(2)}) copy-start(bf16[256,512]{1,0:T(8,128)(2,1)} %nodes.3) | copy-start | bytes 786436
  51.3 2.6 %copy-start.2 = (bf16[256,512]{1,0:T(8,128)(2,1)S(1)}, bf16[256,512]{1,0:T(8,128)(2,1)}, u32[]{:S(2)}) copy-start(bf16[256,512]{1,0:T(8,128)(2,1)} %cotangent.1) | copy-start | bytes 786436
  51.3 2.6 %copy-start.4 = (s32[768]{0:T(1024)S(1)}, s32[768]{0:T(1024)}, u32[]{:S(2)}) copy-start(s32[768]{0:T(1024)} %param.19) | copy-start | bytes 9220
  61.7 25.1 %copy-start.3 = (s32[1,64,8]{1,2,0:T(8,128)S(1)}, s32[1,64,8]{1,2,0:T(8,128)}, u32[]{:S(2)}) copy-start(s32[1,64,8]{1,2,0:T(8,128)} %param.23) | copy-start | bytes 6148
